TPU v7x, 32 devices: a whole 2x2x4 slice. The times are simulated.
32 devices in a mesh: batch: 16 (over z, y, core), seq: 2 (over x).
Axes of the slice: x: 2, y: 2, z: 4, core: 2. Of those that a mesh axis runs over, the one named last changes fastest.
Arguments:
- hidden_in: bfloat16 [1024, 32, 768], P('seq', 'batch'), may hold values from -6 to 6
- memory: bfloat16 [1024, 32, 768], P('seq', 'batch'), may hold values from -6 to 6
- src_len: int32 [32], P('batch'), may hold values from 1 to 1024, as said below
- out_grad: bfloat16 [1024, 32, 768], P('seq', 'batch'), may hold values from -6 to 6
- w_self_qkv: bfloat16 [768, 2304], replicated, may hold values from -0.21875 to 0.21875
- w_self_out: bfloat16 [768, 768], replicated, may hold values from -1.75 to 1.75
- w_cross_q: bfloat16 [768, 768], replicated, may hold values from -0.21875 to 0.21875
- w_cross_kv: bfloat16 [768, 1536], replicated, may hold values from -0.21875 to 0.21875
- w_cross_out: bfloat16 [768, 768], replicated, may hold values from -1.75 to 1.75
- w_ffn_in: bfloat16 [768, 3072], replicated, may hold values from -0.21875 to 0.21875
- w_ffn_out: bfloat16 [3072, 768], replicated, may hold values from -0.109375 to 0.109375
- biases: float32 [7, 768], replicated, may hold values from -1 to 1
- ffn_bias: float32 [3072], replicated, may hold values from -1 to 1
- norm_gain: float32 [3, 768], replicated, may hold values from 0.5 to 1.5
- norm_shift: float32 [3, 768], replicated, may hold values from -1 to 1
Outputs:
- layer_out: bfloat16 [1024, 32, 768], P('seq', 'batch')
- grad_in: float32 [1024, 32, 768], P('seq', 'batch')
- grad_memory: float32 [1024, 32, 768], P('seq', 'batch')
- grad_self_qkv: float32 [768, 2304], P('batch', 'seq')
- grad_self_out: float32 [768, 768], P('batch', 'seq')
- grad_cross_q: float32 [768, 768], P('batch', 'seq')
- grad_cross_kv: float32 [768, 1536], P('batch', 'seq')
- grad_cross_out: float32 [768, 768], P('batch', 'seq')
- grad_ffn_in: float32 [768, 3072], P('batch', 'seq')
- grad_ffn_out: float32 [3072, 768], P('batch', 'seq')
- grad_biases: float32 [7, 768], P(None, 'seq')
- grad_ffn_bias: float32 [3072], P('seq')
- grad_norm_gain: float32 [3, 768], P(None, 'seq')
- grad_norm_shift: float32 [3, 768], P(None, 'seq')
Inputs may be any that keep to these rules, and one draw needn't show every extreme that they name: `src_len`: among the 2 sequences of each index of batch one uses all 1024 source tokens.
All inputs are finite; a program needn't handle non-finite values.
Results may differ from a plain program's by a relative error of at most 0.03.
Values may be sent and summed in bfloat16 or wider, within the bound.
No kernel may reach another device: no remote copies, remote signals or barrier semaphores. Data moves between devices by JAX's collectives and lax.ppermute only.
A program may use at most 448 MiB of HBM per device.

v0:
```python
from functools import partial

import jax
import jax.numpy as jnp
from jax import lax
from jax.sharding import PartitionSpec as P

H = 12


NEGATIVE = -1e30


def from_behind(value, axis, steps):
    count = lax.axis_size(axis)
    pairs = [(source, (source + steps) % count) for source in range(count)]
    return lax.ppermute(value, axis, pairs)


def shifted(block, axis, distance):
    devices = range(lax.axis_size(axis))
    route = [(i - distance, i) for i in devices if i - distance in devices]
    return lax.ppermute(block, axis, route)


def contract_rows(left, right):
    return lax.dot_general(
        left, right, (((0,), (0,)), ((), ())), preferred_element_type=jnp.float32
    )


def times_transposed(grad, weight):
    return lax.dot_general(
        grad, weight, (((1,), (1,)), ((), ())), preferred_element_type=jnp.float32
    )


def norm_forward(value, gain, shift):
    mean = jnp.mean(value, axis=-1, keepdims=True)
    centred = value - mean
    scale = lax.rsqrt(jnp.mean(centred * centred, axis=-1, keepdims=True) + 1e-05)
    unit = centred * scale
    return (unit * gain + shift, unit, scale)


def norm_backward(grad, unit, scale, gain):
    weighted = grad * gain
    inner = (
        weighted
        - jnp.mean(weighted, axis=-1, keepdims=True)
        - unit * jnp.mean(weighted * unit, axis=-1, keepdims=True)
    )
    return (scale * inner, jnp.sum(grad * unit, axis=0), jnp.sum(grad, axis=0))


def allowed_keys(query_pos, key_pos, lengths, causal):
    if causal:
        return (query_pos[:, None] >= key_pos[None, :])[None, None]
    return (key_pos[None, :] < lengths[:, None])[:, None, None, :]


def attend_forward(query, keys, values, lengths, causal, heads):
    span, batch, width = query.shape
    size = width // heads
    query_heads = query.reshape(span, batch, heads, size)
    query_pos = lax.axis_index("seq") * span + lax.iota(jnp.int32, span)

    def block(carry, key_block, value_block, first):
        previous, total, summed = carry
        rows = key_block.shape[0]
        key_pos = first + lax.iota(jnp.int32, rows)
        scores = jnp.einsum(
            "qshd,kshd->shqk",
            query_heads,
            key_block.reshape(rows, batch, heads, size),
            preferred_element_type=jnp.float32,
        )
        allowed = allowed_keys(query_pos, key_pos, lengths, causal)
        top = jnp.maximum(previous, jnp.max(jnp.where(allowed, scores, NEGATIVE), axis=-1))
        weights = jnp.where(allowed, jnp.exp(scores - top[..., None]), 0.0)
        rescale = jnp.exp(previous - top)
        total = total * rescale + jnp.sum(weights, axis=-1)
        summed = summed * rescale[..., None] + jnp.einsum(
            "shqk,kshd->shqd",
            weights.astype(jnp.bfloat16),
            value_block.reshape(rows, batch, heads, size),
            preferred_element_type=jnp.float32,
        )
        return (top, total, summed)

    def fold(carry, piece):
        key_piece, value_piece = piece
        rows = key_piece.shape[0]
        count = rows // span
        firsts = span * lax.iota(jnp.int32, count)

        def inner(state, parts):
            return (block(state, parts[0], parts[1], parts[2]), None)

        carry, unused = lax.scan(
            inner,
            carry,
            (
                key_piece.reshape(count, span, batch, width),
                value_piece.reshape(count, span, batch, width),
                firsts,
            ),
        )
        return carry

    empty = (
        jnp.full((batch, heads, span), NEGATIVE, jnp.float32),
        jnp.zeros((batch, heads, span), jnp.float32),
        jnp.zeros((batch, heads, span, size), jnp.float32),
    )
    if causal:
        top, total, summed = fold(
            empty,
            (
                lax.all_gather(keys, "seq", axis=0, tiled=True),
                lax.all_gather(values, "seq", axis=0, tiled=True),
            ),
        )
    else:
        top, total, summed = fold(
            empty,
            (
                lax.all_gather(keys, "seq", axis=0, tiled=True),
                lax.all_gather(values, "seq", axis=0, tiled=True),
            ),
        )
    mixed = summed / total[..., None]
    mixed = jnp.transpose(mixed, (2, 0, 1, 3)).reshape(span, batch, width)
    return (mixed, top + jnp.log(total))


def block_backward(
    query_heads, grad_heads, delta, logsum, key_block, value_block, allowed, batch, heads, size
):
    span = key_block.shape[0]
    width = heads * size
    key_heads = key_block.reshape(span, batch, heads, size)
    value_heads = value_block.reshape(span, batch, heads, size)
    scores = jnp.einsum(
        "qshd,kshd->shqk", query_heads, key_heads, preferred_element_type=jnp.float32
    )
    weights = jnp.where(allowed, jnp.exp(scores - logsum[..., None]), 0.0)
    grad_weights = jnp.einsum(
        "qshd,kshd->shqk", grad_heads, value_heads, preferred_element_type=jnp.float32
    )
    grad_scores = (weights * (grad_weights - delta[..., None])).astype(jnp.bfloat16)
    grad_query = jnp.einsum(
        "shqk,kshd->qshd", grad_scores, key_heads, preferred_element_type=jnp.float32
    )
    grad_keys = jnp.einsum(
        "shqk,qshd->kshd", grad_scores, query_heads, preferred_element_type=jnp.float32
    ).reshape(span, batch, width)
    grad_values = jnp.einsum(
        "shqk,qshd->kshd",
        weights.astype(jnp.bfloat16),
        grad_heads,
        preferred_element_type=jnp.float32,
    ).reshape(span, batch, width)
    return (grad_query, grad_keys, grad_values)


def attend_backward(query, keys, values, mixed, grad_mixed, logsum, lengths, causal, heads):
    span, batch, width = query.shape
    size = width // heads
    query_heads = query.reshape(span, batch, heads, size)
    grad_heads = grad_mixed.reshape(span, batch, heads, size)
    delta = jnp.sum(
        grad_heads.astype(jnp.float32) * mixed.reshape(span, batch, heads, size), axis=-1
    )
    delta = jnp.transpose(delta, (1, 2, 0))
    devices = lax.axis_size("seq")
    place = lax.axis_index("seq")
    query_pos = place * span + lax.iota(jnp.int32, span)
    grad_query = jnp.zeros((span, batch, heads, size), jnp.float32)
    grad_keys = jnp.zeros((span, batch, width), jnp.float32)
    grad_values = jnp.zeros((span, batch, width), jnp.float32)
    key_block, value_block = (keys, values)
    for step in range(devices):
        owner = (place - step + devices) % devices
        key_pos = owner * span + lax.iota(jnp.int32, span)
        allowed = allowed_keys(query_pos, key_pos, lengths, causal)
        part_query, part_keys, part_values = block_backward(
            query_heads,
            grad_heads,
            delta,
            logsum,
            key_block,
            value_block,
            allowed,
            batch,
            heads,
            size,
        )
        grad_query = grad_query + part_query
        grad_keys = grad_keys + part_keys
        grad_values = grad_values + part_values
        if causal:
            grad_keys, grad_values = (
                from_behind(grad_keys.astype(jnp.bfloat16), "seq", 1).astype(grad_keys.dtype),
                from_behind(grad_values.astype(jnp.bfloat16), "seq", 1).astype(grad_values.dtype),
            )
        else:
            grad_keys, grad_values = (
                from_behind(grad_keys.astype(jnp.bfloat16), "seq", 1).astype(grad_keys.dtype),
                from_behind(grad_values.astype(jnp.bfloat16), "seq", 1).astype(grad_values.dtype),
            )
        if step + 1 < devices:
            if causal:
                key_block, value_block = shifted((key_block, value_block), "seq", 1)
            else:
                key_block, value_block = from_behind((key_block, value_block), "seq", 1)
    return (grad_query.reshape(span, batch, width), grad_keys, grad_values)


def per_device(
    hidden_in,
    memory,
    src_len,
    out_grad,
    w_self_qkv,
    w_self_out,
    w_cross_q,
    w_cross_kv,
    w_cross_out,
    w_ffn_in,
    w_ffn_out,
    biases,
    ffn_bias,
    norm_gain,
    norm_shift,
):
    span, batch, width = hidden_in.shape
    heads = H
    rows = span * batch
    layout = (span, batch, width)
    tokens = hidden_in.reshape(rows, width)
    sources = memory.reshape(rows, width)
    joined = jnp.dot(tokens, w_self_qkv, preferred_element_type=jnp.float32)
    query_self = ((joined[:, :width] + biases[0]) * 0.125).astype(jnp.bfloat16)
    key_self = joined[:, width : 2 * width].astype(jnp.bfloat16)
    value_self = (joined[:, 2 * width :] + biases[1]).astype(jnp.bfloat16)
    mixed_self, logsum_self = attend_forward(
        query_self.reshape(layout),
        key_self.reshape(layout),
        value_self.reshape(layout),
        src_len,
        True,
        heads,
    )
    out_self = mixed_self.reshape(rows, width).astype(jnp.bfloat16)
    resid_one = (
        tokens.astype(jnp.float32)
        + jnp.dot(out_self, w_self_out, preferred_element_type=jnp.float32)
        + biases[2]
    )
    normed_one, unit_one, scale_one = norm_forward(resid_one, norm_gain[0], norm_shift[0])
    normed_one_low = normed_one.astype(jnp.bfloat16)
    query_cross = (
        (jnp.dot(normed_one_low, w_cross_q, preferred_element_type=jnp.float32) + biases[3]) * 0.125
    ).astype(jnp.bfloat16)
    pair = jnp.dot(sources, w_cross_kv, preferred_element_type=jnp.float32)
    key_cross = pair[:, :width].astype(jnp.bfloat16)
    value_cross = (pair[:, width:] + biases[4]).astype(jnp.bfloat16)
    mixed_cross, logsum_cross = attend_forward(
        query_cross.reshape(layout),
        key_cross.reshape(layout),
        value_cross.reshape(layout),
        src_len,
        False,
        heads,
    )
    out_cross = mixed_cross.reshape(rows, width).astype(jnp.bfloat16)
    resid_two = (
        normed_one + jnp.dot(out_cross, w_cross_out, preferred_element_type=jnp.float32) + biases[5]
    )
    normed_two, unit_two, scale_two = norm_forward(resid_two, norm_gain[1], norm_shift[1])
    normed_two_low = normed_two.astype(jnp.bfloat16)
    inner = jnp.dot(normed_two_low, w_ffn_in, preferred_element_type=jnp.float32) + ffn_bias
    active = jax.nn.gelu(inner, approximate=False).astype(jnp.bfloat16)
    resid_three = (
        normed_two + jnp.dot(active, w_ffn_out, preferred_element_type=jnp.float32) + biases[6]
    )
    result, unit_three, scale_three = norm_forward(resid_three, norm_gain[2], norm_shift[2])
    layer_out = result.astype(jnp.bfloat16).reshape(layout)
    grad_three, gain_three, shift_three = norm_backward(
        out_grad.reshape(rows, width).astype(jnp.float32), unit_three, scale_three, norm_gain[2]
    )
    branch_three = grad_three.astype(jnp.bfloat16)
    hidden_pre, hidden_act = (inner, active)
    grad_ffn_out = contract_rows(hidden_act, branch_three)
    grad_act = times_transposed(branch_three, w_ffn_out)
    unused, pull = jax.vjp(partial(jax.nn.gelu, approximate=False), hidden_pre)
    grad_pre = pull(grad_act)[0].astype(jnp.bfloat16)
    grad_ffn_in = contract_rows(normed_two_low, grad_pre)
    grad_normed_two = grad_three + times_transposed(grad_pre, w_ffn_in)
    grad_two, gain_two, shift_two = norm_backward(
        grad_normed_two, unit_two, scale_two, norm_gain[1]
    )
    branch_two = grad_two.astype(jnp.bfloat16)
    grad_cross_out = contract_rows(out_cross, branch_two)
    grad_mixed_cross = times_transposed(branch_two, w_cross_out).astype(jnp.bfloat16)
    raw_query, grad_keys, grad_values = attend_backward(
        query_cross.reshape(layout),
        key_cross.reshape(layout),
        value_cross.reshape(layout),
        mixed_cross,
        grad_mixed_cross.reshape(layout),
        logsum_cross,
        src_len,
        False,
        heads,
    )
    grad_query_cross = (raw_query.reshape(rows, width) * 0.125).astype(jnp.bfloat16)
    grad_pair = jnp.concatenate(
        [
            grad_keys.reshape(rows, width).astype(jnp.bfloat16),
            grad_values.reshape(rows, width).astype(jnp.bfloat16),
        ],
        axis=1,
    )
    grad_cross_q = contract_rows(normed_one_low, grad_query_cross)
    grad_cross_kv = contract_rows(sources, grad_pair)
    grad_memory = times_transposed(grad_pair, w_cross_kv).reshape(layout)
    grad_normed_one = grad_two + times_transposed(grad_query_cross, w_cross_q)
    grad_one, gain_one, shift_one = norm_backward(
        grad_normed_one, unit_one, scale_one, norm_gain[0]
    )
    branch_one = grad_one.astype(jnp.bfloat16)
    grad_self_out = contract_rows(out_self, branch_one)
    grad_mixed_self = times_transposed(branch_one, w_self_out).astype(jnp.bfloat16)
    raw_query, grad_keys, grad_values = attend_backward(
        query_self.reshape(layout),
        key_self.reshape(layout),
        value_self.reshape(layout),
        mixed_self,
        grad_mixed_self.reshape(layout),
        logsum_self,
        src_len,
        True,
        heads,
    )
    grad_joined = jnp.concatenate(
        [
            (raw_query.reshape(rows, width) * 0.125).astype(jnp.bfloat16),
            grad_keys.reshape(rows, width).astype(jnp.bfloat16),
            grad_values.reshape(rows, width).astype(jnp.bfloat16),
        ],
        axis=1,
    )
    grad_self_qkv = contract_rows(tokens, grad_joined)
    grad_in = (grad_one + times_transposed(grad_joined, w_self_qkv)).reshape(layout)
    vector_terms = jnp.stack(
        [
            jnp.sum(grad_joined[:, :width].astype(jnp.float32), axis=0),
            jnp.sum(grad_joined[:, 2 * width :].astype(jnp.float32), axis=0),
            jnp.sum(grad_one, axis=0),
            jnp.sum(grad_query_cross.astype(jnp.float32), axis=0),
            jnp.sum(grad_pair[:, width:].astype(jnp.float32), axis=0),
            jnp.sum(grad_two, axis=0),
            jnp.sum(grad_three, axis=0),
            gain_one,
            gain_two,
            gain_three,
            shift_one,
            shift_two,
            shift_three,
        ]
    )
    bias_terms = jnp.sum(grad_pre.astype(jnp.float32), axis=0)[None]
    (
        grad_self_qkv,
        grad_self_out,
        grad_cross_q,
        grad_cross_kv,
        grad_cross_out,
        grad_ffn_in,
        grad_ffn_out,
        vector_terms,
        bias_terms,
    ) = (
        lax.psum_scatter(
            grad_self_qkv.astype(jnp.bfloat16), "seq", scatter_dimension=1, tiled=True
        ).astype(jnp.float32),
        lax.psum_scatter(
            grad_self_out.astype(jnp.bfloat16), "seq", scatter_dimension=1, tiled=True
        ).astype(jnp.float32),
        lax.psum_scatter(
            grad_cross_q.astype(jnp.bfloat16), "seq", scatter_dimension=1, tiled=True
        ).astype(jnp.float32),
        lax.psum_scatter(
            grad_cross_kv.astype(jnp.bfloat16), "seq", scatter_dimension=1, tiled=True
        ).astype(jnp.float32),
        lax.psum_scatter(
            grad_cross_out.astype(jnp.bfloat16), "seq", scatter_dimension=1, tiled=True
        ).astype(jnp.float32),
        lax.psum_scatter(
            grad_ffn_in.astype(jnp.bfloat16), "seq", scatter_dimension=1, tiled=True
        ).astype(jnp.float32),
        lax.psum_scatter(
            grad_ffn_out.astype(jnp.bfloat16), "seq", scatter_dimension=1, tiled=True
        ).astype(jnp.float32),
        lax.psum_scatter(
            vector_terms.astype(jnp.bfloat16), "seq", scatter_dimension=1, tiled=True
        ).astype(jnp.float32),
        lax.psum_scatter(
            bias_terms.astype(jnp.bfloat16), "seq", scatter_dimension=1, tiled=True
        ).astype(jnp.float32),
    )
    (
        grad_self_qkv,
        grad_self_out,
        grad_cross_q,
        grad_cross_kv,
        grad_cross_out,
        grad_ffn_in,
        grad_ffn_out,
    ) = (
        lax.psum_scatter(
            grad_self_qkv.astype(jnp.bfloat16), "batch", scatter_dimension=0, tiled=True
        ).astype(jnp.float32),
        lax.psum_scatter(
            grad_self_out.astype(jnp.bfloat16), "batch", scatter_dimension=0, tiled=True
        ).astype(jnp.float32),
        lax.psum_scatter(
            grad_cross_q.astype(jnp.bfloat16), "batch", scatter_dimension=0, tiled=True
        ).astype(jnp.float32),
        lax.psum_scatter(
            grad_cross_kv.astype(jnp.bfloat16), "batch", scatter_dimension=0, tiled=True
        ).astype(jnp.float32),
        lax.psum_scatter(
            grad_cross_out.astype(jnp.bfloat16), "batch", scatter_dimension=0, tiled=True
        ).astype(jnp.float32),
        lax.psum_scatter(
            grad_ffn_in.astype(jnp.bfloat16), "batch", scatter_dimension=0, tiled=True
        ).astype(jnp.float32),
        lax.psum_scatter(
            grad_ffn_out.astype(jnp.bfloat16), "batch", scatter_dimension=0, tiled=True
        ).astype(jnp.float32),
    )
    vector_terms, bias_terms = lax.psum((vector_terms, bias_terms), "batch")
    return (
        layer_out,
        grad_in,
        grad_memory,
        grad_self_qkv,
        grad_self_out,
        grad_cross_q,
        grad_cross_kv,
        grad_cross_out,
        grad_ffn_in,
        grad_ffn_out,
        vector_terms[0:7],
        bias_terms[0],
        vector_terms[7:10],
        vector_terms[10:13],
    )


def solution(mesh):
    in_specs = (
        P("seq", "batch", None),
        P("seq", "batch", None),
        P("batch"),
        P("seq", "batch", None),
        P(),
        P(),
        P(),
        P(),
        P(),
        P(),
        P(),
        P(),
        P(),
        P(),
        P(),
    )
    out_specs = (
        P("seq", "batch", None),
        P("seq", "batch", None),
        P("seq", "batch", None),
        P("batch", "seq"),
        P("batch", "seq"),
        P("batch", "seq"),
        P("batch", "seq"),
        P("batch", "seq"),
        P("batch", "seq"),
        P("batch", "seq"),
        P(None, "seq"),
        P("seq"),
        P(None, "seq"),
        P(None, "seq"),
    )
    return jax.shard_map(
        per_device, mesh=mesh, in_specs=in_specs, out_specs=out_specs, check_vma=False
    )
```

profile of v0, /device:TPU:8, one launch (start us, length us, event | category | flops | bytes accessed | tf_op | source)
XLA Modules:
  0.0 1898.5 jit_solution(18087369547562702057)
XLA Ops:
  139.7 13.6 fusion.103
  155.2 140.2 %collective-permute-done = bf16[512,2,768]{2,1,0:T(2,128)(2,1)} collective-permute-done((bf16[512,2,768]{2,1,0:T(2,128)(2,1)}, bf16[512,2,768]{2,1,0:T(2,128)(2,1)}, u32[]{:S(2)}, u32[]{:S(2)}) %collective-permute-start) | collective-permute-done | bytes 1572896 | tf_op jit(solution)/shard_map/ppermute | solution.py:17
  310.1 13.6 fusion.105
  328.7 104.7 %while.30 = (s32[]{:T(128)}, f32[2,12,512]{2,1,0:T(8,128)}, f32[2,12,512]{2,1,0:T(8,128)}, f32[2,12,512,64]{2,3,1,0:T(8,128)}, s32[2]{0:T(128)S(1)}, /*index=5*/...) while((s32[]{:T(128)}, f32[2,12,512]{2,1,0:T(8,128)}, ...), condition=%wide.region_3.4_spmd.clone, body=%wide.region_0.3_spmd.clone.sunk | while | flops 1663628288 | bytes 101916952 | solution.py:100
  337.3 14.4 fusion.198
  352.6 10.8 fusion.199
  367.4 12.6 fusion.201
  389.1 14.4 fusion.198
  404.4 10.8 fusion.199
  419.2 13.5 fusion.201
  435.3 8.7 copy.241
  444.0 6.9 bitcast_convert_fusion.5
  477.2 104.8 %while.31 = (s32[]{:T(128)}, f32[2,12,512]{2,1,0:T(8,128)}, f32[2,12,512]{2,1,0:T(8,128)}, f32[2,12,512,64]{2,3,1,0:T(8,128)}, s32[2]{0:T(128)S(1)}, /*index=5*/...) while((s32[]{:T(128)}, f32[2,12,512]{2,1,0:T(8,128)}, ...), condition=%wide.region_9.10_spmd.clone, body=%wide.region_6.9_spmd.clone.sunk | while | flops 1663366656 | bytes 100868384 | solution.py:100
  485.3 15.4 select_reduce_fusion.2
  501.6 10.7 bitcast_reduce_fusion.2
  516.2 12.5 fusion.206
  537.0 15.4 select_reduce_fusion.2
  553.4 10.7 bitcast_reduce_fusion.2
  568.0 13.4 fusion.206
  582.0 8.7 copy.248
  611.2 34.8 %multiply_convert_fusion.4 = (bf16[1024,3072]{1,0:T(8,128)(2,1)S(1)}, f32[1024,3072]{1,0:T(8,128)}, f32[1024,3072]{1,0:T(8,128)}) fusion(f32[3072]{0:T(1024)S(1)} %copy-done.89, bf16[768,3072]{1,0:T(8,128)(2,1)S(1)} %bitcast.239, f32[1024,768]{1,0:T(8,128)S(1)} %get-tuple-element.436, f32[768]{0:T(1024)S(1)} %copy-done.82, f32[768]{0:T(1024)S(1)} %copy-done.66, ...), kind=kOutput, calls=%fused_computation.70 | convolution fusion | flops 5043388416 | bytes 39348224 | tf_op jit(solution)/shard_map/dot_general | solution.py:283
  658.6 19.2 %fusion.97 = (bf16[3072]{0:T(1024)(128)(2,1)}, bf16[1024,3072]{1,0:T(8,128)(2,1)}) fusion(f32[1024,3072]{1,0:T(8,128)} %get-tuple-element.413, bf16[3072,768]{1,0:T(8,128)(2,1)} %param.29, f32[1024,768]{1,0:T(8,128)} %get-tuple-element.407, f32[1024,3072]{1,0:T(8,128)} %get-tuple-element.437, f32[3072]{0:T(1024)S(1)} %copy-done.89), kind=kOutput, calls=%fused_computation.220 | convolution fusion | flops 4882953216 | bytes 39340032 | tf_op jit(solution)/shard_map/dot_general | solution.py:33
  677.8 11.6 multiply_reduce_fusion.1
  706.8 8.7 fusion.54
  716.1 10.6 fusion.102
  726.7 10.1 fusion.100
  738.6 12.6 fusion.33
  751.2 11.8 fusion.66
  763.0 15.2 multiply_convert_fusion.2
  778.2 16.9 multiply_convert_fusion.3
  795.1 10.2 fusion.101
  805.4 11.1 fusion.96
  816.5 7.4 copy.259
  853.7 8.9 fusion.55
  875.2 12.3 fusion.69
  892.6 13.1 fusion.29
  911.1 9.1 fusion.107
  923.7 8.4 convolution_convert_fusion.4
  944.2 24.8 %multiply_convert_fusion.1 = bf16[2,12,512,512]{3,2,1,0:T(8,128)(2,1)} fusion(f32[2,12,512,512]{3,2,1,0:T(8,128)} %fusion.103, f32[2,12,512]{2,1,0:T(8,128)} %copy.264, f32[2,12,512]{2,1,0:T(8,128)} %copy-done.46, pred[512,512]{1,0:T(8,128)(4,1)} %get-tuple-element.430, bf16[512,2,12,64]{0,3,2,1:T(8,128)(2,1)} %copy.262, ...), kind=kOutput, calls=%fused_computation.45 | convolution fusion | flops 836763648 | bytes 41254912 | tf_op jit(solution)/shard_map/qshd,kshd->shqk/dot_general | solution.py:148
  968.9 8.0 convolution_convert_fusion.5
  991.8 17.9 collective-permute-done.8
  1015.2 16.5 multiply_convert_fusion
  1031.7 50.9 %collective-permute-done.11 = bf16[512,2,768]{2,0,1:T(8,128)(2,1)S(1)} collective-permute-done((bf16[512,2,768]{2,0,1:T(8,128)(2,1)S(1)}, bf16[512,2,768]{2,0,1:T(8,128)(2,1)S(1)}, u32[]{:S(2)}, u32[]{:S(2)}) %collective-permute-start.11) | collective-permute-done | bytes 1572896 | tf_op jit(solution)/shard_map/ppermute | solution.py:17
  1091.1 23.5 %collective-permute-done.9 = bf16[512,2,768]{2,0,1:T(8,128)(2,1)} collective-permute-done((bf16[512,2,768]{2,0,1:T(8,128)(2,1)}, bf16[512,2,768]{2,0,1:T(8,128)(2,1)}, u32[]{:S(2)}, u32[]{:S(2)}) %collective-permute-start.9) | collective-permute-done | bytes 1572896 | tf_op jit(solution)/shard_map/ppermute | solution.py:17
  1131.1 9.1 fusion.106
  1153.1 10.2 fusion.104
  1163.3 10.5 fusion.95
  1173.8 7.4 copy.270
  1190.0 10.1 collective-permute-done.7
  1209.5 23.7 %collective-permute-done.5 = bf16[512,2,768]{2,0,1:T(8,128)(2,1)} collective-permute-done((bf16[512,2,768]{2,0,1:T(8,128)(2,1)}, bf16[512,2,768]{2,0,1:T(8,128)(2,1)}, u32[]{:S(2)}, u32[]{:S(2)}) %collective-permute-start.5) | collective-permute-done | bytes 1572896 | tf_op jit(solution)/shard_map/ppermute | solution.py:17
  1246.2 7.8 fusion.56
  1254.7 10.5 convolution_convert_fusion.1
  1265.3 9.6 convolution_convert_fusion
  1321.8 42.4 %reduce-scatter.43.cloned.1.call-done = bf16[768,1536]{1,0:T(8,128)(2,1)} async-done(((bf16[768,3072]{1,0:T(8,128)(2,1)}), bf16[768,1536]{1,0:T(8,128)(2,1)}) %reduce-scatter.43.cloned.1.call-update) | async-done | bytes 2359312 | tf_op jit(solution)/shard_map/reduce_scatter | solution.py:401
  1364.2 62.3 %reduce-scatter.59.cloned.1.call-done = bf16[384,3072]{1,0:T(8,128)(2,1)} async-done(((bf16[768,3072]{1,0:T(8,128)(2,1)}), bf16[384,3072]{1,0:T(8,128)(2,1)}) %reduce-scatter.59.cloned.1.call-update) | async-done | bytes 2359312
  1435.3 11.4 reduce-scatter.63.cloned.1.call-done
  1460.6 8.2 convolution_add_fusion.2
  1474.9 53.4 %all-reduce = (f32[13,384]{1,0:T(8,128)}, f32[1536]{0:T(1024)}) all-reduce(bf16[13,384]{1,0:T(8,128)(2,1)S(1)} %copy.308, f32[1536]{0:T(1024)} %convert_reduce_fusion), channel_id=1, replica_groups=mesh['batch'=16,'seq'=2] {'batch'}, use_global_device_ids=true, to_apply=%region_50.51 | all-reduce | flops 6528 | bytes 42240 | tf_op jit(solution)/shard_map/psum | solution.py:445
  1532.5 44.0 %reduce-scatter.35.cloned.1.call-done = bf16[48,384]{1,0:T(8,128)(2,1)} async-done(((bf16[768,384]{1,0:T(8,128)(2,1)}), bf16[48,384]{1,0:T(8,128)(2,1)}) %reduce-scatter.35.cloned.1.call-update) | async-done | bytes 36880 | tf_op jit(solution)/shard_map/reduce_scatter | solution.py:426
  1577.9 55.9 %reduce-scatter.41.cloned.1.call-done = bf16[48,384]{1,0:T(8,128)(2,1)} async-done(((bf16[768,384]{1,0:T(8,128)(2,1)}), bf16[48,384]{1,0:T(8,128)(2,1)}) %reduce-scatter.41.cloned.1.call-update) | async-done | bytes 36880 | tf_op jit(solution)/shard_map/reduce_scatter | solution.py:435
  1635.2 59.6 %reduce-scatter.55.cloned.1.call-done = bf16[48,768]{1,0:T(8,128)(2,1)} async-done(((bf16[768,768]{1,0:T(8,128)(2,1)}), bf16[48,768]{1,0:T(8,128)(2,1)}) %reduce-scatter.55.cloned.1.call-update) | async-done | bytes 73744
  1698.1 59.7 %reduce-scatter.49.cloned.1.call-done = bf16[48,1152]{1,0:T(8,128)(2,1)} async-done(((bf16[768,1152]{1,0:T(8,128)(2,1)}), bf16[48,1152]{1,0:T(8,128)(2,1)}) %reduce-scatter.49.cloned.1.call-update) | async-done | bytes 110608
  1761.4 62.8 %reduce-scatter.45.cloned.1.call-done = bf16[48,1536]{1,0:T(8,128)(2,1)} async-done(((bf16[768,1536]{1,0:T(8,128)(2,1)}), bf16[48,1536]{1,0:T(8,128)(2,1)}) %reduce-scatter.45.cloned.1.call-update) | async-done | bytes 147472 | tf_op jit(solution)/shard_map/reduce_scatter | solution.py:438
  1825.9 64.0 %reduce-scatter.47.cloned.1.call-done = bf16[192,384]{1,0:T(8,128)(2,1)} async-done(((bf16[3072,384]{1,0:T(8,128)(2,1)}), bf16[192,384]{1,0:T(8,128)(2,1)}) %reduce-scatter.47.cloned.1.call-update) | async-done | bytes 147472 | tf_op jit(solution)/shard_map/reduce_scatter | solution.py:441
  (480 shorter events, 539.9 us)
Async XLA Ops:
  7.2 321.5 %all-gather.7.cloned.1.call-start = ((), (), s32[]{:S(2)}) async-start(), calls=%async_computation.17 | async-start | bytes 4718592 | tf_op jit(solution)/shard_map/all_gather | solution.py:121
  30.7 298.0 %all-gather.5.cloned.1.call-start = ((), (), s32[]{:S(2)}) async-start(), calls=%async_computation.16 | async-start | bytes 4718592 | tf_op jit(solution)/shard_map/all_gather | solution.py:120
  41.4 435.8 %all-gather.11.cloned.1.call-start = ((), (), s32[]{:S(2)}) async-start(), calls=%async_computation.19 | async-start | bytes 4718592 | tf_op jit(solution)/shard_map/all_gather | solution.py:129
  62.7 414.5 %all-gather.9.cloned.1.call-start = ((), (), s32[]{:S(2)}) async-start(), calls=%async_computation.18 | async-start | bytes 4718592 | tf_op jit(solution)/shard_map/all_gather | solution.py:128
  62.7 237.6 %collective-permute-start.1 = (bf16[512,2,768]{2,1,0:T(2,128)(2,1)}, bf16[512,2,768]{2,1,0:T(2,128)(2,1)}, u32[]{:S(2)}, u32[]{:S(2)}) collective-permute-start(bf16[512,2,768]{2,1,0:T(2,128)(2,1)} %reshape.408), channel_id=1, source_target_pairs={{0,1},{1,0},{2,3},{3,2},{4,5},{5,4},{6,7},{7,6},{8,9},{9,8},{10,11... | collective-permute-start | bytes 4718600 | tf_op jit(solution)/shard_map/ppermute | solution.py:17
  64.3 240.9 %collective-permute-start.2 = (bf16[512,2,768]{2,1,0:T(2,128)(2,1)}, bf16[512,2,768]{2,1,0:T(2,128)(2,1)}, u32[]{:S(2)}, u32[]{:S(2)}) collective-permute-start(bf16[512,2,768]{2,1,0:T(2,128)(2,1)} %reshape.401), channel_id=1, source_target_pairs={{0,1},{2,3},{4,5},{6,7},{8,9},{10,11},{12,13},{14,15},{16,17},{18,... | collective-permute-start | bytes 4718600 | tf_op jit(solution)/shard_map/ppermute | solution.py:23
  68.0 255.8 %collective-permute-start.3 = (bf16[512,2,768]{2,1,0:T(2,128)(2,1)}, bf16[512,2,768]{2,1,0:T(2,128)(2,1)}, u32[]{:S(2)}, u32[]{:S(2)}) collective-permute-start(bf16[512,2,768]{2,1,0:T(2,128)(2,1)} %reshape.403), channel_id=1, source_target_pairs={{0,1},{2,3},{4,5},{6,7},{8,9},{10,11},{12,13},{14,15},{16,17},{18,... | collective-permute-start | bytes 4718600 | tf_op jit(solution)/shard_map/ppermute | solution.py:23
  78.1 217.2 %collective-permute-start = (bf16[512,2,768]{2,1,0:T(2,128)(2,1)}, bf16[512,2,768]{2,1,0:T(2,128)(2,1)}, u32[]{:S(2)}, u32[]{:S(2)}) collective-permute-start(bf16[512,2,768]{2,1,0:T(2,128)(2,1)} %reshape.406), channel_id=1, source_target_pairs={{0,1},{1,0},{2,3},{3,2},{4,5},{5,4},{6,7},{7,6},{8,9},{9,8},{10,11... | collective-permute-start | bytes 4718600 | tf_op jit(solution)/shard_map/ppermute | solution.py:17
  80.9 1227.5 %reduce-scatter.53.cloned.1.call-start = ((), (), s32[]{:S(2)}) async-start(), calls=%async_computation.30 | async-start | bytes 1769472
  139.7 13.7 copy-start.58
  352.6 10.9 copy-start.3
  367.4 12.6 copy-start.4
  404.4 10.9 copy-start.3
  419.2 13.5 copy-start.4
  516.2 12.5 copy-start.6
  568.0 13.4 copy-start.6
  605.8 40.2 %slice-start = ((s8[4718592]{0:T(1024)(128)(4,1)}), s8[4194304]{0:T(1024)(128)(4,1)S(1)}, s32[]{:S(2)}) async-start(s8[4718592]{0:T(1024)(128)(4,1)} %bitcast.236), calls=%async_computation.36 | async-start | bytes 8388608
  610.5 35.6 %copy-start.16 = (f32[1024,768]{1,0:T(8,128)}, f32[1024,768]{1,0:T(8,128)S(1)}, u32[]{:S(2)}) copy-start(f32[1024,768]{1,0:T(8,128)S(1)} %get-tuple-element.436) | copy-start | bytes 9437188
  610.5 78.9 %copy-start.53 = (f32[1024]{0:T(1024)}, f32[1024]{0:T(1024)S(1)}, u32[]{:S(2)}) copy-start(f32[1024]{0:T(1024)S(1)} %broadcast_multiply_fusion.7) | copy-start | bytes 12292
  611.1 78.4 %copy-start.61 = (f32[1024]{0:T(1024)}, f32[1024]{0:T(1024)S(1)}, u32[]{:S(2)}) copy-start(f32[1024]{0:T(1024)S(1)} %add_rsqrt_fusion.1) | copy-start | bytes 12292
  611.2 34.8 %copy-start.78 = (f32[768]{0:T(1024)S(1)}, f32[768]{0:T(1024)}, u32[]{:S(2)}) copy-start(f32[768]{0:T(1024)} %get-tuple-element.351) | copy-start | bytes 9220
  611.2 34.8 %slice-start.1 = ((s8[4718592]{0:T(1024)(128)(4,1)}), s8[524288]{0:T(1024)(128)(4,1)S(1)}, s32[]{:S(2)}) async-start(s8[4718592]{0:T(1024)(128)(4,1)} %bitcast.236), calls=%async_computation.37 | async-start | bytes 1048576
  677.8 11.6 copy-start.17
  726.7 11.9 copy-start.60
  738.6 12.6 copy-start.25
  738.6 12.6 copy-start.48
  738.6 12.6 copy-start.85
  751.2 11.8 copy-start.43
  751.2 11.8 copy-start.50
  763.0 15.2 copy-start.30
  778.2 16.9 copy-start.13
  871.8 115.0 %collective-permute-start.10 = (bf16[512,2,768]{2,0,1:T(8,128)(2,1)}, bf16[512,2,768]{2,0,1:T(8,128)(2,1)}, u32[]{:S(2)}, u32[]{:S(2)}) collective-permute-start(bf16[512,2,768]{2,0,1:T(8,128)(2,1)} %copy.287), channel_id=1, source_target_pairs={{0,1},{1,0},{2,3},{3,2},{4,5},{5,4},{6,7},{7,6},{8,9},{9,8},{10,11... | collective-permute-start | bytes 4718600 | tf_op jit(solution)/shard_map/ppermute | solution.py:17
  875.2 12.3 copy-start.46
  890.1 253.8 %collective-permute-start.6 = (bf16[512,2,768]{2,0,1:T(8,128)(2,1)}, bf16[512,2,768]{2,0,1:T(8,128)(2,1)}, u32[]{:S(2)}, u32[]{:S(2)}) collective-permute-start(bf16[512,2,768]{2,0,1:T(8,128)(2,1)} %copy.277), channel_id=1, source_target_pairs={{0,1},{1,0},{2,3},{3,2},{4,5},{5,4},{6,7},{7,6},{8,9},{9,8},{10,11... | collective-permute-start | bytes 4718600 | tf_op jit(solution)/shard_map/ppermute | solution.py:17
  892.6 418.1 %reduce-scatter.51.cloned.1.call-start = ((), (), s32[]{:S(2)}) async-start(), calls=%async_computation.29 | async-start | bytes 1769472
  934.7 75.0 %collective-permute-start.8 = (bf16[512,2,768]{2,0,1:T(8,128)(2,1)}, bf16[512,2,768]{2,0,1:T(8,128)(2,1)}, u32[]{:S(2)}, u32[]{:S(2)}) collective-permute-start(bf16[512,2,768]{2,0,1:T(8,128)(2,1)} %copy.282), channel_id=1, source_target_pairs={{0,1},{1,0},{2,3},{3,2},{4,5},{5,4},{6,7},{7,6},{8,9},{9,8},{10,11... | collective-permute-start | bytes 4718600 | tf_op jit(solution)/shard_map/ppermute | solution.py:17
  944.1 368.9 %reduce-scatter.57.cloned.1.call-start = ((), (), s32[]{:S(2)}) async-start(), calls=%async_computation.32 | async-start | bytes 1769472
  944.2 24.8 %copy-start.1 = (bf16[512,2,12,64]{0,3,2,1:T(8,128)(2,1)S(1)}, bf16[512,2,12,64]{0,3,2,1:T(8,128)(2,1)}, u32[]{:S(2)}) copy-start(bf16[512,2,12,64]{0,3,2,1:T(8,128)(2,1)} %get-tuple-element.677) | copy-start | bytes 4718596
  979.5 170.2 %collective-permute-start.4 = (bf16[512,2,768]{2,0,1:T(8,128)(2,1)}, bf16[512,2,768]{2,0,1:T(8,128)(2,1)}, u32[]{:S(2)}, u32[]{:S(2)}) collective-permute-start(bf16[512,2,768]{2,0,1:T(8,128)(2,1)} %copy.272), channel_id=1, source_target_pairs={{0,1},{1,0},{2,3},{3,2},{4,5},{5,4},{6,7},{7,6},{8,9},{9,8},{10,11... | collective-permute-start | bytes 4718600 | tf_op jit(solution)/shard_map/ppermute | solution.py:17
  986.7 328.5 %reduce-scatter.39.cloned.1.call-start = ((), (), s32[]{:S(2)}) async-start(), calls=%async_computation.23 | async-start | bytes 3538944 | tf_op jit(solution)/shard_map/reduce_scatter | solution.py:395
  986.8 22.9 %copy-start.14 = (f32[512,2,768]{2,0,1:T(8,128)S(1)}, f32[512,2,768]{2,0,1:T(8,128)}, u32[]{:S(2)}) copy-start(f32[512,2,768]{2,0,1:T(8,128)} %copy.284) | copy-start | bytes 9437188
  989.7 25.5 %copy-start.29 = (bf16[512,2,12,64]{0,3,2,1:T(8,128)(2,1)S(1)}, bf16[512,2,12,64]{0,3,2,1:T(8,128)(2,1)}, u32[]{:S(2)}) copy-start(bf16[512,2,12,64]{0,3,2,1:T(8,128)(2,1)} %copy.262) | copy-start | bytes 4718596
  989.7 25.5 %copy-start.39 = (pred[512,512]{1,0:T(8,128)(4,1)S(1)}, pred[512,512]{1,0:T(8,128)(4,1)}, u32[]{:S(2)}) copy-start(pred[512,512]{1,0:T(8,128)(4,1)} %get-tuple-element.429) | copy-start | bytes 786436
  989.7 25.5 %copy-start.42 = (bf16[512,2,768]{0,2,1:T(8,128)(2,1)S(1)}, bf16[512,2,768]{0,2,1:T(8,128)(2,1)}, u32[]{:S(2)}) copy-start(bf16[512,2,768]{0,2,1:T(8,128)(2,1)} %copy.268) | copy-start | bytes 4718596
  989.7 25.5 %copy-start.47 = (f32[2,12,512]{2,1,0:T(8,128)S(1)}, f32[2,12,512]{2,1,0:T(8,128)}, u32[]{:S(2)}) copy-start(f32[2,12,512]{2,1,0:T(8,128)} %copy-done.46) | copy-start | bytes 147460
  989.7 25.5 %copy-start.49 = (f32[2,12,512]{2,1,0:T(8,128)S(1)}, f32[2,12,512]{2,1,0:T(8,128)}, u32[]{:S(2)}) copy-start(f32[2,12,512]{2,1,0:T(8,128)} %copy.264) | copy-start | bytes 147460
  989.7 92.9 %collective-permute-start.11 = (bf16[512,2,768]{2,0,1:T(8,128)(2,1)S(1)}, bf16[512,2,768]{2,0,1:T(8,128)(2,1)S(1)}, u32[]{:S(2)}, u32[]{:S(2)}) collective-permute-start(bf16[512,2,768]{2,0,1:T(8,128)(2,1)S(1)} %add_convert_fusion.1), channel_id=1, source_target_pairs={{0,1},{1,0},{2,3},{3,2},{4,5},{5,4},{6,7},{7,6},{8,9},{9,8},{10,11... | collective-permute-start | bytes 4718600 | tf_op jit(solution)/shard_map/ppermute | solution.py:17
  1012.7 101.9 %collective-permute-start.9 = (bf16[512,2,768]{2,0,1:T(8,128)(2,1)}, bf16[512,2,768]{2,0,1:T(8,128)(2,1)}, u32[]{:S(2)}, u32[]{:S(2)}) collective-permute-start(bf16[512,2,768]{2,0,1:T(8,128)(2,1)} %add_convert_fusion.2), channel_id=1, source_target_pairs={{0,1},{1,0},{2,3},{3,2},{4,5},{5,4},{6,7},{7,6},{8,9},{9,8},{10,11... | collective-permute-start | bytes 4718600 | tf_op jit(solution)/shard_map/ppermute | solution.py:17
  1131.0 186.7 %reduce-scatter.33.cloned.1.call-start = ((), (), s32[]{:S(2)}) async-start(), calls=%async_computation.20 | async-start | bytes 5308416 | tf_op jit(solution)/shard_map/reduce_scatter | solution.py:386
  1148.0 52.2 %collective-permute-start.7 = (bf16[512,2,768]{2,0,1:T(8,128)(2,1)}, bf16[512,2,768]{2,0,1:T(8,128)(2,1)}, u32[]{:S(2)}, u32[]{:S(2)}) collective-permute-start(bf16[512,2,768]{2,0,1:T(8,128)(2,1)} %add_convert_fusion.3), channel_id=1, source_target_pairs={{0,1},{1,0},{2,3},{3,2},{4,5},{5,4},{6,7},{7,6},{8,9},{9,8},{10,11... | collective-permute-start | bytes 4718600 | tf_op jit(solution)/shard_map/ppermute | solution.py:17
  1152.7 80.4 %collective-permute-start.5 = (bf16[512,2,768]{2,0,1:T(8,128)(2,1)}, bf16[512,2,768]{2,0,1:T(8,128)(2,1)}, u32[]{:S(2)}, u32[]{:S(2)}) collective-permute-start(bf16[512,2,768]{2,0,1:T(8,128)(2,1)} %add_convert_fusion.4), channel_id=1, source_target_pairs={{0,1},{1,0},{2,3},{3,2},{4,5},{5,4},{6,7},{7,6},{8,9},{9,8},{10,11... | collective-permute-start | bytes 4718600 | tf_op jit(solution)/shard_map/ppermute | solution.py:17
  1254.0 110.1 %reduce-scatter.43.cloned.1.call-start = ((), (), s32[]{:S(2)}) async-start(), calls=%async_computation.25 | async-start | bytes 7077888 | tf_op jit(solution)/shard_map/reduce_scatter | solution.py:401
  1265.2 161.3 %reduce-scatter.59.cloned.1.call-start = ((), (), s32[]{:S(2)}) async-start(), calls=%async_computation.33 | async-start | bytes 7077888
  1281.7 165.1 %reduce-scatter.63.cloned.1.call-start = ((), (), s32[]{:S(2)}) async-start(), calls=%async_computation.35 | async-start | bytes 1179648
  1283.8 190.2 %reduce-scatter.61.cloned.1.call-start = ((), (), s32[]{:S(2)}) async-start(), calls=%async_computation.34 | async-start | bytes 294912
  1287.4 16.6 copy-start.74
  1290.6 13.4 copy-start.75
  1308.4 222.7 %reduce-scatter.37.cloned.1.call-start = ((), (), s32[]{:S(2)}) async-start(), calls=%async_computation.22 | async-start | bytes 626688 | tf_op jit(solution)/shard_map/reduce_scatter | solution.py:429
  1310.6 265.8 %reduce-scatter.35.cloned.1.call-start = ((), (), s32[]{:S(2)}) async-start(), calls=%async_computation.21 | async-start | bytes 626688 | tf_op jit(solution)/shard_map/reduce_scatter | solution.py:426
  1312.9 320.8 %reduce-scatter.41.cloned.1.call-start = ((), (), s32[]{:S(2)}) async-start(), calls=%async_computation.24 | async-start | bytes 626688 | tf_op jit(solution)/shard_map/reduce_scatter | solution.py:435
  1315.2 379.5 %reduce-scatter.55.cloned.1.call-start = ((), (), s32[]{:S(2)}) async-start(), calls=%async_computation.31 | async-start | bytes 1253376
  1317.7 440.2 %reduce-scatter.49.cloned.1.call-start = ((), (), s32[]{:S(2)}) async-start(), calls=%async_computation.28 | async-start | bytes 1880064
  1321.7 502.5 %reduce-scatter.45.cloned.1.call-start = ((), (), s32[]{:S(2)}) async-start(), calls=%async_computation.26 | async-start | bytes 2506752 | tf_op jit(solution)/shard_map/reduce_scatter | solution.py:438
  1364.2 525.7 %reduce-scatter.47.cloned.1.call-start = ((), (), s32[]{:S(2)}) async-start(), calls=%async_computation.27 | async-start | bytes 2506752 | tf_op jit(solution)/shard_map/reduce_scatter | solution.py:441
  (73 other events, 375.5 us)
Sparse Core Ops, SparseCore 0:
  30.8 57.1 all-gather.6
  89.6 78.4 all-gather.4
  169.7 76.7 all-gather.10
  247.8 62.9 all-gather.8
  892.7 35.9 reduce-scatter.52
  944.2 34.5 reduce-scatter.50
  986.9 35.9 reduce-scatter.56
  1131.1 51.5 reduce-scatter.38
  1254.2 47.6 reduce-scatter.32
  1304.1 59.9 reduce-scatter.42
  1366.5 59.9 reduce-scatter.58
  1429.3 17.4 reduce-scatter.62
  1449.6 10.9 reduce-scatter.60
  1464.0 54.7 reduce-scatter.36
  1522.5 53.8 reduce-scatter.34
  1579.9 53.8 reduce-scatter.40
  1637.7 57.0 reduce-scatter.54
  1698.8 58.9 reduce-scatter.48
  1762.1 62.1 reduce-scatter.44
  1827.9 61.9 reduce-scatter.46
where the time goes:
time: 1910 us; the launch traced here: 1900 us
  waiting for transfers between devices  729 us (38%)
  matrix products  523 us (27%)
  local copies, waits for them, and re-layouts  422 us (22%)
  other arithmetic  135 us (7%)
  blocking collectives  53.4 us (3%)
  starting transfers between devices  20.4 us (1%)
    ppermute x10, waiting for transfers between devices, from_behind(): return lax.ppermute(value, axis, pairs)  266 us
    unnamed x28, waiting for transfers between devices  193 us
    unnamed x193, local copies, waits for them, and re-layouts  77.1 us
    dot_general x4, matrix products, block_backward(): jnp.einsum('qshd,kshd->shqk', grad_heads, value_heads, preferred_element_...  73.3 us
    reduce_scatter x1, waiting for transfers between devices, per_device(): lax.psum_scatter(grad_ffn_out.astype(jnp.bfloat16), 'batch', scatter_dime...  64 us
    reduce_scatter x1, waiting for transfers between devices, per_device(): lax.psum_scatter(grad_ffn_in.astype(jnp.bfloat16), 'batch', scatter_dimen...  62.8 us
    dot_general x4, matrix products, block(): jnp.einsum('qshd,kshd->shqk', query_heads, key_block.reshape(rows, batch,...  59.7 us
    dot_general x7, matrix products, times_transposed(): lax.dot_general(grad, weight, (((1,), (1,)), ((), ())), preferred_element...  57.6 us
  transfers between devices with their start and end apart: 32, of which 15 were waited for; matrix products, arithmetic and copies ran while one was open for 34% of the time, Pallas kernels for 0%

commit v1 on v0

--- a/solution.py
+++ b/solution.py
@@ -1,8 +1,11 @@
+import functools
 from functools import partial
 
 import jax
 import jax.numpy as jnp
 from jax import lax
+from jax.experimental import pallas as pl
+from jax.experimental.pallas import tpu as pltpu
 from jax.sharding import PartitionSpec as P
 
 H = 12
@@ -217,7 +220,7 @@
     return (grad_query.reshape(span, batch, width), grad_keys, grad_values)
 
 
-def per_device(
+def per_device_general(
     hidden_in,
     memory,
     src_len,
@@ -461,7 +464,962 @@
     )
 
 
+LOG2E = 1.4426950408889634
+NN = (((1,), (0,)), ((), ()))
+NT = (((1,), (1,)), ((), ()))
+HD = 64
+BIG = -1e30
+f32, bf16 = jnp.float32, jnp.bfloat16
+
+def dot(a, b, dims=NN):
+    return lax.dot_general(a, b, dims, preferred_element_type=f32)
+
+def lanes(shape):
+    return lax.broadcasted_iota(jnp.int32, shape, len(shape) - 1)
+
+def swap_halves(x):
+    return jnp.concatenate([x[:, HD:], x[:, :HD]], axis=1)
+
+def fwd_kernel(len_ref, q_ref, k_ref, v_ref, o_ref, lp_ref, acc_ref, *, causal, heads, qb, ahead):
+    p = pl.program_id(0)
+    n = q_ref.shape[0]
+    nk = k_ref.shape[0]
+    scaled = q_ref[...].astype(f32) * LOG2E
+    hi = scaled.astype(bf16)
+    lo = (scaled - hi.astype(f32)).astype(bf16)
+    first = lanes((n, 128)) < HD
+    hi_s, lo_s = swap_halves(hi), swap_halves(lo)
+    q_aug = (jnp.where(first, hi, lo_s), jnp.where(first, hi_s, lo))
+    kk = k_ref[...]
+    k_s = swap_halves(kk)
+    k_aug = [jnp.where(first, kk, k_s), jnp.where(first, k_s, kk)]
+    if not causal:
+        length = len_ref[0]
+        row = lax.broadcasted_iota(jnp.int32, (nk, 128), 0)
+        extra = jnp.where((row >= length) & (lanes((nk, 128)) == 0), BIG, 0.0).astype(bf16)
+        k_aug = [jnp.concatenate([x, extra], axis=1) for x in k_aug]
+        one = (lanes((n, 128)) == 0).astype(bf16)
+        q_aug = [jnp.concatenate([x, one], axis=1) for x in q_aug]
+    vt = jnp.transpose(v_ref[...])
+    ones = jnp.ones((16, nk), bf16)
+    va = [jnp.concatenate([vt[h * HD:(h + 1) * HD], ones], axis=0) for h in range(2)]
+
+    def scores(c, h):
+        top_k = (c + 1) * qb if causal else nk
+        s = dot(k_aug[h][:top_k], q_aug[h][c * qb:(c + 1) * qb], NT)
+        if causal:
+            r = lax.broadcasted_iota(jnp.int32, (qb, qb), 0)
+            d = jnp.where(r <= lanes((qb, qb)), s[c * qb:], BIG)
+            s = jnp.concatenate([s[:c * qb], d], axis=0) if c else d
+        return s
+
+    steps = [(c, h) for c in range(n // qb) for h in range(2)]
+    queue = [scores(*x) for x in steps[:ahead]]
+    parts = []
+    for i, (c, h) in enumerate(steps):
+        if i + ahead < len(steps):
+            queue.append(scores(*steps[i + ahead]))
+        s = queue.pop(0)
+        m = jnp.max(s, axis=0, keepdims=True)
+        pt = jnp.exp2(s - m).astype(bf16)
+        ot = dot(va[h][:, :s.shape[0]], pt)
+        l = ot[HD:HD + 1]
+        parts.append(ot[:HD] * (1.0 / l))
+        acc_ref[pl.ds(2 * p + h, 1), c * qb:(c + 1) * qb] = m + jnp.log2(l)
+        if h == 1:
+            o_ref[c * qb:(c + 1) * qb, :] = jnp.transpose(jnp.concatenate(parts, axis=0)).astype(bf16)
+            parts = []
+
+    @pl.when(p == pl.num_programs(0) - 1)
+    def _():
+        rows = acc_ref[...]
+        wide = jnp.concatenate([rows, jnp.zeros((128 - rows.shape[0], n), f32)], axis=0)
+        cols = jnp.transpose(wide)
+        a = cols.astype(bf16)
+        cols = cols - a.astype(f32)
+        b = cols.astype(bf16)
+        c = (cols - b.astype(f32)).astype(bf16)
+        lane = lanes((n, 128))
+        sh = lambda x, k: jnp.concatenate([jnp.zeros((n, k), bf16), x[:, :128 - k]], axis=1)
+        out = jnp.where(lane < 16, a, jnp.where(lane < 32, sh(b, 16), jnp.where(lane < 48, sh(c, 32), jnp.where(lane == 127, 1.0, 0.0).astype(bf16))))
+        lp_ref[...] = out
+
+def attn_fwd(length, q, k, v, causal, qb=256, ahead=2):
+    n, d = q.shape
+    blk = lambda r: pl.BlockSpec((r, 128), lambda p, l: (0, p))
+    return pl.pallas_call(
+        functools.partial(fwd_kernel, causal=causal, heads=d // HD, qb=qb, ahead=ahead),
+        grid_spec=pltpu.PrefetchScalarGridSpec(
+            num_scalar_prefetch=1, grid=(d // 128,),
+            in_specs=[blk(n), blk(k.shape[0]), blk(k.shape[0])],
+            out_specs=[blk(n), pl.BlockSpec((n, 128), lambda p, l: (0, 0))],
+            scratch_shapes=[pltpu.VMEM((16, n), f32)]),
+        out_shape=[pltpu.HBM((n, d), bf16), pltpu.HBM((n, 128), bf16)],
+        compiler_params=params(40),
+        cost_estimate=cost((n + 256) * n * 1024 // (2 if causal else 1) * (d // HD), 8 * n * d, n * n * d // HD),
+        name="attn_fwd",
+    )(length, *hbm(q, k, v))
+
+def side_rows(kind, refs, own):
+    if kind == "early":
+        one, cross_a, cross_b, ffn, bias = refs
+        both = lambda r: jnp.concatenate([cross_a[r : r + 1, :], cross_b[r : r + 1, :]], axis=1)
+        rows = [one[2:3, :], both(0), both(1), ffn[5:6, :], ffn[2:3, :], one[0:1, :], ffn[3:4, :], ffn[0:1, :], one[1:2, :], ffn[4:5, :], ffn[1:2, :]]
+        half = rows[0].shape[1] // 2
+        wide = bias.shape[1] // 2
+        sides = []
+        for x in range(2):
+            sides += [r[:, x * half : (x + 1) * half] for r in rows]
+            sides += [bias[0:1, x * wide + c * half : x * wide + (c + 1) * half] for c in range(wide // half)]
+            sides += [jnp.zeros((1, half), f32)] * (16 - len(rows) - wide // half)
+        return jnp.concatenate(sides, axis=0).astype(bf16)
+    rows = [refs[0][0:2, :], refs[1][0:2, :], own[0:2, :], jnp.zeros((10, own.shape[1]), f32)]
+    rows = jnp.concatenate(rows, axis=0)
+    return jnp.concatenate([rows, jnp.zeros((16, 128), f32)], axis=1).astype(bf16)
+
+
+def bwd_kernel(len_ref, q_ref, k_ref, v_ref, o_ref, g_ref, lp_ref, *rest, causal, qb, first_pair, stride, unit, kind):
+    if unit:
+        place, tok_ref, *side, out_ref, sums_ref, send_ref, own_ref = rest
+    else:
+        out_ref, sums_ref = rest
+    p = pl.program_id(0) * stride + first_pair
+    n, nk = q_ref.shape[0], k_ref.shape[0]
+    first = lanes((n, 128)) < HD
+    q = q_ref[...]
+    scaled = q.astype(f32) * LOG2E
+    hi = scaled.astype(bf16)
+    lo = (scaled - hi.astype(f32)).astype(bf16)
+    hi_s, lo_s = swap_halves(hi), swap_halves(lo)
+    lp = lp_ref[...]
+    q_aug = [jnp.concatenate([x, lp], axis=1) for x in (jnp.where(first, hi, lo_s), jnp.where(first, hi_s, lo))]
+    kk = k_ref[...]
+    k_s = swap_halves(kk)
+    v = v_ref[...]
+    lane = lanes((nk, 128))
+    g = g_ref[...]
+    zero = jnp.zeros((), bf16)
+    go = g.astype(f32) * o_ref[...].astype(f32)
+    go_hi = go.astype(bf16)
+    go_lo = (go - go_hi.astype(f32)).astype(bf16)
+    br = lax.broadcasted_iota(jnp.int32, (128, 128), 0)
+    bl = lanes((128, 128))
+    pick = jnp.where(((bl < 3) & (br < HD)) | ((bl >= 3) & (bl < 6) & (br >= HD)), 1.0, 0.0).astype(bf16)
+    dl = dot(go_hi, pick) + dot(go_lo, pick)
+    da = dl.astype(bf16)
+    rest = dl - da.astype(f32)
+    db = rest.astype(bf16)
+    dc = (rest - db.astype(f32)).astype(bf16)
+    part = lanes((n, 128))
+    part = jnp.where(part >= 3, part - 3, part)
+    dpack = jnp.where(part == 0, da, jnp.where(part == 1, db, dc))
+    g_aug = jnp.concatenate([g, dpack], axis=1)
+    qt = jnp.transpose(q)
+    gt = jnp.transpose(g)
+    minus = jnp.full((), -1.0, bf16)
+    row = lax.broadcasted_iota(jnp.int32, (nk, 128), 0)
+    dq_parts, dkts, dvts = [], [], []
+    for h in range(2):
+        head = 2 * p + h
+        sel = jnp.where((lane < 48) & ((lane & 15) == head), -1.0, 0.0)
+        if not causal:
+            sel = jnp.where((lane == 127) & (row >= len_ref[0]), BIG, sel)
+        k_aug = jnp.concatenate([jnp.where(first, kk, k_s) if h == 0 else jnp.where(first, k_s, kk), sel.astype(bf16)], axis=1)
+        dsel = jnp.where((lane >= 3 * h) & (lane < 3 * h + 3), -1.0, 0.0).astype(bf16)
+        v_m = jnp.where(first, v, zero) if h == 0 else jnp.where(first, zero, v)
+        v_aug = jnp.concatenate([v_m, dsel], axis=1)
+        parts = []
+        dkt = jnp.zeros((HD, nk), f32)
+        dvt = jnp.zeros((HD, nk), f32)
+        for c in range(n // qb):
+            rows = slice(c * qb, (c + 1) * qb)
+            top_k = (c + 1) * qb if causal else nk
+            s = dot(q_aug[h][rows], k_aug[:top_k], NT)
+            w = jnp.exp2(s)
+            if causal:
+                r = lax.broadcasted_iota(jnp.int32, (qb, qb), 0)
+                dg = jnp.where(r >= lanes((qb, qb)), w[:, c * qb:], 0.0)
+                w = jnp.concatenate([w[:, :c * qb], dg], axis=1) if c else dg
+            dp = dot(g_aug[rows], v_aug[:top_k], NT)
+            ds = (w * dp).astype(bf16)
+            wb = w.astype(bf16)
+            a = dot(gt[h * HD:(h + 1) * HD, rows], wb)
+            b = dot(qt[h * HD:(h + 1) * HD, rows], ds)
+            if top_k < nk:
+                pad = jnp.zeros((HD, nk - top_k), f32)
+                a = jnp.concatenate([a, pad], axis=1)
+                b = jnp.concatenate([b, pad], axis=1)
+            dvt = dvt + a
+            dkt = dkt + b
+            parts.append(dot(ds, kk[:top_k]))
+        dq_parts.append(parts)
+        dkts.append(dkt)
+        dvts.append(dvt)
+    sums = jnp.zeros((1, 128), f32)
+    dqs = []
+    for c in range(n // qb):
+        rows = slice(c * qb, (c + 1) * qb)
+        fl = lanes((qb, 128)) < HD
+        dq = (jnp.where(fl, dq_parts[0][c], dq_parts[1][c]) * 0.125).astype(bf16)
+        dqs.append(dq)
+        sums = sums + jnp.sum(dq.astype(f32), axis=0, keepdims=True)
+    dk = jnp.transpose(jnp.concatenate(dkts, axis=0)).astype(bf16)
+    dv = jnp.transpose(jnp.concatenate(dvts, axis=0)).astype(bf16)
+    v_sums = jnp.sum(dv.astype(f32), axis=0, keepdims=True)
+    grads = (jnp.concatenate(dqs, axis=0), dk, dv)
+    if not unit:
+        sums_ref[...] = jnp.concatenate([sums, v_sums, jnp.zeros((6, 128), f32)], axis=0)
+        for m, part in enumerate(grads):
+            out_ref[m] = part
+        return
+    for at in range(2):
+        @pl.when(pl.program_id(0) == at)
+        def _(at=at):
+            cols = slice(at * 128, (at + 1) * 128)
+            sums_ref[:, cols] = jnp.concatenate([sums, v_sums, jnp.zeros((6, 128), f32)], axis=0)
+            for m, part in enumerate(grads):
+                out_ref[m, :, cols] = part
+
+    @pl.when(pl.program_id(0) == 1)
+    def _():
+        joined = jnp.concatenate([out_ref[0], out_ref[1], out_ref[2]], axis=1)
+        store_units(place, dot(tok_ref[...], joined, TN).astype(bf16), unit, send_ref, own_ref)
+        if kind:
+            rows = side_rows(kind, side, sums_ref[...])
+            for ref in (send_ref, own_ref):
+                for y in range(2):
+                    for x in range(2):
+                        for z in range(ref.shape[2]):
+                            ref[y, x, z, unit:] = rows
+
+
+def attn_bwd(length, q, k, v, o, g, lp, causal, first, stride, count, tokens=None, place=None, nb=0, kind="", side=(), qb=256):
+    n, d = q.shape
+    blk = pl.BlockSpec((n, 128), lambda p, l: (0, first + stride * p))
+    ins = [blk] * 5 + [pl.BlockSpec((n, 128), lambda p, l: (0, 0))]
+    outs = [pl.BlockSpec((3, n, 128), lambda p, l: (0, 0, p)), pl.BlockSpec((8, 128), lambda p, l: (0, p))]
+    shapes = [pltpu.HBM((3, n, count * 128), bf16), pltpu.HBM((8, count * 128), f32)]
+    args = hbm(q, k, v, o, g, lp)
+    unit = 0
+    if tokens is not None:
+        unit = d // nb
+        rows = unit + {"early": 32, "late": 16, "": 0}[kind]
+        ins += [pl.BlockSpec(memory_space=pltpu.SMEM), pl.BlockSpec((n, d), lambda p, l: (0, 0))]
+        ins += [pl.BlockSpec(s.shape, lambda p, l: (0, 0)) for s in side]
+        args += [place] + hbm(tokens, *side)
+        outs = [pl.BlockSpec((3, n, 256), lambda p, l: (0, 0, 0)), pl.BlockSpec((8, 256), lambda p, l: (0, 0))]
+        outs += [pl.BlockSpec((2, 2, nb // 4, rows, 384), lambda p, l: (0, 0, 0, 0, 0))] * 2
+        shapes += [pltpu.HBM((2, 2, nb // 4, rows, 384), bf16)] * 2
+    return pl.pallas_call(
+        functools.partial(bwd_kernel, causal=causal, qb=qb, first_pair=first, stride=stride, unit=unit, kind=kind),
+        grid_spec=pltpu.PrefetchScalarGridSpec(
+            num_scalar_prefetch=1, grid=(count,), in_specs=ins, out_specs=outs),
+        out_shape=shapes,
+        compiler_params=params(40),
+        cost_estimate=cost((n + 256) * n * 2560 // (2 if causal else 1) * count * 2, 16 * n * count * 128, 2 * n * n * count),
+        name="attn_bwd",
+    )(length, *args)
+
+
+def cost(flops, moved, exps=0):
+    return pl.CostEstimate(flops=int(flops), bytes_accessed=int(moved), transcendentals=int(exps))
+
+
+def params(mib):
+    return pltpu.CompilerParams(vmem_limit_bytes=mib * 2**20)
+
+
+def hbm(*values):
+    return [pltpu.with_memory_space_constraint(v, pltpu.HBM) for v in values]
+
+
+def whole():
+    return pl.BlockSpec(memory_space=pltpu.VMEM)
+
+
+def fixed(shape):
+    return pl.BlockSpec(shape, lambda *_: (0,) * len(shape), pipeline_mode=pl.Buffered(1))
+
+
+def spread_rows(block):
+    return lambda i, *_: (i, 0)
+
+
+def project_kernel(place, mine, got, weight, biases, *outs, step, plan):
+    i = pl.program_id(0)
+    x = jnp.where(i // step == place[0], mine[...], got[...])
+    outs[0][...] = x
+    joined = dot(x, weight[...])
+    width = x.shape[1]
+    for n, (bias, scale) in enumerate(plan):
+        part = joined[:, n * width : (n + 1) * width]
+        if bias is not None:
+            part = part + biases[bias : bias + 1, :]
+        if scale != 1.0:
+            part = part * scale
+        outs[n + 1][...] = part.astype(bf16)
+
+
+def project(place, pairs, got, weight, biases, plan, rows=256):
+    half, width = got.shape
+    step = half // rows
+    cols = weight.shape[1]
+    block = pl.BlockSpec((rows, width), lambda i, p: (i, 0))
+    return pl.pallas_call(
+        functools.partial(project_kernel, step=step, plan=plan),
+        grid_spec=pltpu.PrefetchScalarGridSpec(
+            num_scalar_prefetch=1,
+            grid=(2 * step,),
+            in_specs=[
+                pl.BlockSpec((rows, width), lambda i, p: (i % step, p[0])),
+                pl.BlockSpec((rows, width), lambda i, p: (i % step, 0)),
+                whole(),
+                whole(),
+            ],
+            out_specs=[block] * (1 + len(plan)),
+        ),
+        out_shape=[pltpu.HBM((2 * half, width), bf16)] * (1 + len(plan)),
+        compiler_params=params(32),
+        cost_estimate=cost(4 * half * width * cols, 2 * width * cols + 12 * half * width),
+        name="project",
+    )(place, *hbm(pairs, got), weight, biases)
+
+
+def norm_unit(value):
+    mean = jnp.mean(value, axis=-1, keepdims=True)
+    centred = value - mean
+    scale = lax.rsqrt(jnp.mean(centred * centred, axis=-1, keepdims=True) + 1e-05)
+    return centred * scale, scale
+
+
+def norm_back(grad, unit, scale, gain):
+    weighted = grad * gain
+    return scale * (
+        weighted
+        - jnp.mean(weighted, axis=-1, keepdims=True)
+        - unit * jnp.mean(weighted * unit, axis=-1, keepdims=True)
+    )
+
+
+def row_sum(value):
+    return jnp.sum(value, axis=0, keepdims=True)
+
+
+def after_self_kernel(o, tok, w_out, w_q, biases, gain, shift, unit_ref, scale_ref, low_ref, q_ref):
+    resid = tok[...].astype(f32) + dot(o[...], w_out[...]) + biases[2:3, :]
+    unit, scale = norm_unit(resid)
+    unit_ref[...] = unit
+    scale_ref[...] = jnp.broadcast_to(scale, scale_ref.shape)
+    low_ = (unit * gain[0:1, :] + shift[0:1, :]).astype(bf16)
+    low_ref[...] = low_
+    q_ref[...] = ((dot(low_, w_q[...]) + biases[3:4, :]) * 0.125).astype(bf16)
+
+
+def after_self(o, tok, w_out, w_q, biases, gain, shift, rows=256):
+    n, d = o.shape
+    block = pl.BlockSpec((rows, d), lambda i: (i, 0))
+    return pl.pallas_call(
+        after_self_kernel,
+        grid=(n // rows,),
+        in_specs=[block, block, whole(), whole()] + [whole()] * 3,
+        out_specs=[block, pl.BlockSpec((rows, 128), lambda i: (i, 0)), block, block],
+        out_shape=[
+            pltpu.HBM((n, d), f32),
+            pltpu.HBM((n, 128), f32),
+            pltpu.HBM((n, d), bf16),
+            pltpu.HBM((n, d), bf16),
+        ],
+        compiler_params=params(32),
+        cost_estimate=cost(4 * n * d * d, 4 * d * d + 12 * n * d),
+        name="after_self",
+    )(*hbm(o, tok), w_out, w_q, biases, gain, shift)
+
+
+RATE = 0.3275911 * 0.7071067811865476
+TAIL = tuple(0.5 * c for c in (0.254829592, -0.284496736, 1.421413741, -1.453152027, 1.061405429))
+DENSITY = 0.3989422804014327
+
+
+def gelu_pair(v):
+    size = jnp.abs(v)
+    base = 1.0 + RATE * size
+    t = pl.reciprocal(base, approx=True)
+    t = t * (2.0 - base * t)
+    poly = TAIL[4]
+    for c in TAIL[3::-1]:
+        poly = c + t * poly
+    bell = jnp.exp2((v * v) * (-0.5 * LOG2E))
+    tail = t * poly * bell
+    below = jnp.where(v >= 0.0, 1.0 - tail, tail)
+    return v * below, below + v * (DENSITY * bell)
+
+
+def ffn_kernel(
+    o, unit_one, cot, w_co, w_in, w_out, biases, ffn_bias, gain, shift,
+    layer_ref, act_ref, pre_ref, low_ref, b3_ref, g2_ref, b2_ref, gm_ref, sums_ref, fsum_ref,
+    slope, *, chunk,
+):
+    i = pl.program_id(0)
+    ff = w_in.shape[1]
+    n_chunks = ff // chunk
+
+    @pl.when(i == 0)
+    def _():
+        sums_ref[...] = jnp.zeros_like(sums_ref)
+        fsum_ref[...] = jnp.zeros_like(fsum_ref)
+
+    normed_one = unit_one[...] * gain[0:1, :] + shift[0:1, :]
+    resid = normed_one + dot(o[...], w_co[...]) + biases[5:6, :]
+    unit_two, scale_two = norm_unit(resid)
+    normed_two = unit_two * gain[1:2, :] + shift[1:2, :]
+    low_two = normed_two.astype(bf16)
+    low_ref[...] = low_two
+
+    def inner(j):
+        at = slice(j * chunk, (j + 1) * chunk)
+        return dot(low_two, w_in[:, at]) + ffn_bias[0:1, at]
+
+    total = normed_two + biases[6:7, :]
+    ahead = inner(0)
+    for j in range(n_chunks):
+        v = ahead
+        if j + 1 < n_chunks:
+            ahead = inner(j + 1)
+        at = slice(j * chunk, (j + 1) * chunk)
+        act, grad = gelu_pair(v)
+        act = act.astype(bf16)
+        act_ref[:, at] = act
+        slope[:, at] = grad
+        total = total + dot(act, w_out[at, :])
+    unit, scale = norm_unit(total)
+    layer_ref[...] = (unit * gain[2:3, :] + shift[2:3, :]).astype(bf16)
+    g = cot[...].astype(f32)
+    grad_three = norm_back(g, unit, scale, gain[2:3, :])
+    branch = grad_three.astype(bf16)
+    b3_ref[...] = branch
+    sums_ref[0:1, :] += row_sum(g * unit)
+    sums_ref[1:2, :] += row_sum(g)
+    sums_ref[2:3, :] += row_sum(grad_three)
+
+    def back(j):
+        return dot(branch, w_out[j * chunk : (j + 1) * chunk, :], NT)
+
+    total = grad_three
+    ahead = back(0)
+    for j in range(n_chunks):
+        v = ahead
+        if j + 1 < n_chunks:
+            ahead = back(j + 1)
+        at = slice(j * chunk, (j + 1) * chunk)
+        pre = (v * slope[:, at]).astype(bf16)
+        pre_ref[:, at] = pre
+        fsum_ref[0:1, at] += row_sum(pre.astype(f32))
+        total = total + dot(pre, w_in[:, at], NT)
+    grad_two = norm_back(total, unit_two, scale_two, gain[1:2, :])
+    g2_ref[...] = grad_two
+    branch = grad_two.astype(bf16)
+    b2_ref[...] = branch
+    sums_ref[3:4, :] += row_sum(total * unit_two)
+    sums_ref[4:5, :] += row_sum(total)
+    sums_ref[5:6, :] += row_sum(grad_two)
+    gm_ref[...] = dot(branch, w_co[...], NT).astype(bf16)
+
+
+def ffn(o, unit_one, cot, w_co, w_in, w_out, biases, ffn_bias, gain, shift, rows=256, chunk=512):
+    n, d = o.shape
+    ff = w_in.shape[1]
+    block = pl.BlockSpec((rows, d), lambda i: (i, 0))
+    wide = pl.BlockSpec((rows, ff), lambda i: (i, 0))
+    low_shape = pltpu.HBM((n, d), bf16)
+    return pl.pallas_call(
+        functools.partial(ffn_kernel, chunk=chunk),
+        grid=(n // rows,),
+        in_specs=[block, block, block, whole(), whole(), whole()] + [whole()] * 4,
+        out_specs=[block, wide, wide, block, block, block, block, block,
+                   pl.BlockSpec((8, d), lambda i: (0, 0)), pl.BlockSpec((8, ff), lambda i: (0, 0))],
+        out_shape=[
+            low_shape,
+            pltpu.HBM((n, ff), bf16),
+            pltpu.HBM((n, ff), bf16),
+            low_shape,
+            low_shape,
+            pltpu.HBM((n, d), f32),
+            low_shape,
+            low_shape,
+            pltpu.HBM((8, d), f32),
+            pltpu.HBM((8, ff), f32),
+        ],
+        scratch_shapes=[pltpu.VMEM((rows, ff), f32)],
+        compiler_params=params(48),
+        cost_estimate=cost(8 * n * d * ff + 4 * n * d * d, 4 * d * ff + 4 * n * ff + 20 * n * d, 2 * n * ff),
+        name="ffn",
+    )(*hbm(o, unit_one, cot), w_co, w_in, w_out, biases, ffn_bias, gain, shift)
+
+
+def before_self_kernel(g2, gqa, gqb, unit_ref, scale_ref, w_q, w_out, gain, g1_ref, b1_ref, gm_ref, gq_ref, sums_ref):
+    @pl.when(pl.program_id(0) == 0)
+    def _():
+        sums_ref[...] = jnp.zeros_like(sums_ref)
+
+    gq = jnp.concatenate([gqa[0], gqb[0]], axis=1)
+    gq_ref[...] = gq
+    g = g2[...] + dot(gq, w_q[...], NT)
+    unit = unit_ref[...]
+    grad = norm_back(g, unit, scale_ref[:, 0:1], gain[0:1, :])
+    g1_ref[...] = grad
+    branch = grad.astype(bf16)
+    b1_ref[...] = branch
+    sums_ref[0:1, :] += row_sum(g * unit)
+    sums_ref[1:2, :] += row_sum(g)
+    sums_ref[2:3, :] += row_sum(grad)
+    gm_ref[...] = dot(branch, w_out[...], NT).astype(bf16)
+
+
+def before_self(g2, gqa, gqb, unit, scale, w_q, w_out, gain, rows=256):
+    n, d = g2.shape
+    block = pl.BlockSpec((rows, d), lambda i: (i, 0))
+    return pl.pallas_call(
+        before_self_kernel,
+        grid=(n // rows,),
+        in_specs=[block, pl.BlockSpec((1, rows, d // 2), lambda i: (0, i, 0)), pl.BlockSpec((1, rows, d // 2), lambda i: (0, i, 0)), block, pl.BlockSpec((rows, 128), lambda i: (i, 0)), whole(), whole(), whole()],
+        out_specs=[block, block, block, block, pl.BlockSpec((8, d), lambda i: (0, 0))],
+        out_shape=[
+            pltpu.HBM((n, d), f32),
+            pltpu.HBM((n, d), bf16),
+            pltpu.HBM((n, d), bf16),
+            pltpu.HBM((n, d), bf16),
+            pltpu.HBM((8, d), f32),
+        ],
+        compiler_params=params(32),
+        cost_estimate=cost(4 * n * d * d, 4 * d * d + 18 * n * d),
+        name="before_self",
+    )(*hbm(g2, gqa, gqb, unit, scale), w_q, w_out, gain)
+
+
+TN = (((0,), (0,)), ((), ()))
+
+
+def store_units(place, value, unit, send_ref, own_ref, first=0, z_local=False):
+    mx, mz, my, core = place[0], place[1], place[2], place[3]
+    half = value.shape[1] // 2
+    for mine in range(2):
+        @pl.when(core == mine)
+        def _():
+            for u in range(value.shape[0] // unit):
+                ref = own_ref if u % 2 == mine else send_ref
+                z = 0 if z_local else jnp.bitwise_xor(u // 4, mz)
+                y = jnp.bitwise_xor((u // 2) % 2, my)
+                for x in range(2):
+                    ref[y, jnp.bitwise_xor(x, mx), z, :unit] = value[u * unit : (u + 1) * unit, x * half : (x + 1) * half]
+
+
+def tall_kernel(place, a, b, send_ref, own_ref, *, unit):
+    value = dot(a[...], b[...], TN).astype(bf16)
+    store_units(place, value, unit, send_ref, own_ref, z_local=True)
+
+
+def tall_grad(place, a, b, nb):
+    n, rows = a.shape
+    cols = b.shape[1]
+    nz = nb // 4
+    unit = rows // nb
+    out = pltpu.HBM((2, 2, nz, unit, cols // 2), bf16)
+    spec = pl.BlockSpec((2, 2, 1, unit, cols // 2), lambda z, p: (0, 0, jnp.bitwise_xor(z, p[1]), 0, 0))
+    return pl.pallas_call(
+        functools.partial(tall_kernel, unit=unit),
+        grid_spec=pltpu.PrefetchScalarGridSpec(
+            num_scalar_prefetch=1,
+            grid=(nz,),
+            in_specs=[pl.BlockSpec((n, rows // nz), lambda z, p: (0, z)), pl.BlockSpec((n, cols), lambda z, p: (0, 0))],
+            out_specs=[spec, spec],
+        ),
+        out_shape=[out, out],
+        compiler_params=params(24),
+        cost_estimate=cost(2 * n * rows * cols, 2 * (n * rows + n * cols + rows * cols)),
+        name="tall_grad",
+    )(place, *hbm(a, b))
+
+
+def wide_kernel(place, *refs, steps, unit):
+    send_ref, own_ref = refs[-2:]
+    j = pl.program_id(0)
+    for a_at, left, right, first, count in steps:
+        @pl.when((j >= first) & (j < first + count))
+        def _(a_at=a_at, left=left, right=right):
+            flat = lambda r: refs[r][...].reshape(refs[r].shape[-2:])
+            value = dot(refs[a_at][...], jnp.concatenate([flat(left), flat(right)], axis=1), TN).astype(bf16)
+            store_units(place, value, unit, send_ref, own_ref)
+
+
+def wide_grad(place, terms, nb, block=384):
+    n, rows = terms[0][0].shape
+    unit = rows // nb
+    arrays, specs, steps, first = [], [], [], 0
+    whole_a = pl.BlockSpec((n, rows), lambda j, p: (0, 0))
+    for a, b, leads in terms:
+        if not any(a is other for other in arrays):
+            arrays.append(a)
+            specs.append(whole_a)
+        a_at = next(i for i, other in enumerate(arrays) if other is a)
+        count = b.shape[-1] // block // (1 if leads else 2)
+        for side in range(2):
+            def where(j, p, first=first, count=count, side=side, leads=leads):
+                inside = jnp.clip(j - first, 0, count - 1)
+                return (leads[side], 0, inside) if leads else (0, side * count + inside)
+            arrays.append(b)
+            specs.append(pl.BlockSpec((1, n, block) if leads else (n, block), where))
+        steps.append((a_at, len(arrays) - 2, len(arrays) - 1, first, count))
+        first += count
+    steps = [(a, l, r, f, c) for a, l, r, f, c in steps]
+    out = pltpu.HBM((2, 2, nb // 4, unit, first * block), bf16)
+    spec = pl.BlockSpec((2, 2, nb // 4, unit, block), lambda j, p: (0, 0, 0, 0, j))
+    return pl.pallas_call(
+        functools.partial(wide_kernel, steps=steps, unit=unit),
+        grid_spec=pltpu.PrefetchScalarGridSpec(
+            num_scalar_prefetch=1, grid=(first,), in_specs=specs, out_specs=[spec, spec]
+        ),
+        out_shape=[out, out],
+        compiler_params=params(40),
+        cost_estimate=cost(4 * n * rows * first * block, 4 * rows * first * block + 4 * n * first * block),
+        name="wide_grad",
+    )(place, *hbm(*arrays))
+
+
+def grad_rows_kernel(place, *refs, columns, based):
+    gs, weight = refs[: len(columns)], refs[len(columns)]
+    out_ref = refs[-1]
+    value = None
+    for g, chunks in zip(gs, columns):
+        for m, starts in enumerate(chunks):
+            if not starts:
+                continue
+            w = [weight[:, s : s + size] for s, size in starts]
+            w = w[0] if len(w) == 1 else jnp.concatenate(w, axis=1)
+            term = dot(g[m], w, NT)
+            value = term if value is None else value + term
+    if based:
+        value = value + refs[len(columns) + 1][...]
+
+    out_ref[...] = value.astype(out_ref.dtype)
+
+
+def grad_rows(place, terms, columns, weight, base, mine, rows=256):
+    n = terms[0].shape[1]
+    d, k = weight.shape
+    steps = n // 2 // rows
+    half = lambda i, p: (p[0] if mine else 1 - p[0]) * steps + i
+    ins = [pl.BlockSpec((t.shape[0], rows, t.shape[2]), lambda i, p: (0, half(i, p), 0)) for t in terms] + [whole()]
+    args = hbm(*terms) + [weight]
+    if base is not None:
+        ins.append(pl.BlockSpec((rows, d), lambda i, p: (half(i, p), 0)))
+        args += hbm(base)
+    return pl.pallas_call(
+        functools.partial(grad_rows_kernel, columns=columns, based=base is not None),
+        grid_spec=pltpu.PrefetchScalarGridSpec(
+            num_scalar_prefetch=1,
+            grid=(steps,),
+            in_specs=ins,
+            out_specs=pl.BlockSpec((rows, d), lambda i, p: (i, 0)),
+        ),
+        out_shape=pltpu.HBM((n // 2, d), f32 if mine else bf16),
+        compiler_params=params(40),
+        cost_estimate=cost(n * k * d, n * k + 2 * k * d + 4 * n * d),
+        name="grad_rows",
+    )(place, *args)
+
+
+def route(nb, move):
+    dz, dy, dc, dx = move
+    pairs = []
+    for b in range(nb):
+        z, y, core = b // 4, (b // 2) % 2, b % 2
+        for x in range(2):
+            target = (z ^ dz) * 4 + (y ^ dy) * 2 + (core ^ dc)
+            pairs.append((b * 2 + x, target * 2 + (x ^ dx)))
+    return pairs
+
+
+def send(value, nb, move):
+    return lax.ppermute(value, ("batch", "seq"), route(nb, move))
+
+
+def core_stage(buffers, nb):
+    to_send, own = buffers
+    return own, send(to_send, nb, (0, 0, 1, 0))
+
+
+def y_prepare(state):
+    own, got = state
+    return (own[1].astype(f32) + got[1].astype(f32)).astype(bf16), (own, got)
+
+
+def y_move(value, nb):
+    return send(value, nb, (0, 1, 0, 0))
+
+
+def x_prepare(state):
+    own, got, more = state
+    total = own[0].astype(f32) + got[0].astype(f32) + more.astype(f32)
+    return total[0].astype(bf16), total[1].astype(bf16)
+
+
+def x_move(value, nb):
+    return send(value, nb, (0, 0, 0, 1))
+
+
+def z_prepare(state):
+    kept, got = state
+    total = kept.astype(f32) + got.astype(f32)
+    return total[0::2].astype(bf16), total[1::2].astype(bf16)
+
+
+def z_move(value, nb, bit):
+    return send(value, nb, (1 << bit, 0, 0, 0))
+
+
+def after_y(state):
+    own, got, more = state
+    return (own[0].astype(f32) + got[0].astype(f32) + more.astype(f32)).astype(bf16)
+
+
+def direct_z(total, nb):
+    result = total[:, 0].astype(f32)
+    for d in range(1, nb // 4):
+        result = result + send(total[:, d], nb, (d, 0, 0, 0)).astype(f32)
+    return result
+
+
+def at(value, index, axis):
+    return lax.dynamic_index_in_dim(value, index, axis, keepdims=False)
+
+
+def last_stage(state):
+    kept, got = state
+    return (kept.astype(f32) + got.astype(f32))[0]
+
+
+def tie(*values):
+    return lax.optimization_barrier(values)
+
+
+def swap(value):
+    return lax.ppermute(value, "seq", [(0, 1), (1, 0)])
+
+
+def split_pairs(local):
+    positions, _, width = local.shape
+    pairs = local.reshape(positions, 2 * width)
+    x = lax.axis_index("seq")
+    return pairs, lax.dynamic_slice(pairs, (0, (1 - x) * width), (positions, width))
+
+
+def join_pairs(mine, got):
+    x = lax.axis_index("seq")
+    got = got.astype(mine.dtype)
+    both = jnp.concatenate([jnp.where(x == 0, mine, got), jnp.where(x == 0, got, mine)], axis=1)
+    return both.reshape(mine.shape[0], 2, mine.shape[1])
+
+
+def whole_sequence(pairs, got):
+    x = lax.axis_index("seq")
+    width = got.shape[1]
+    mine = lax.dynamic_slice(pairs, (0, x * width), got.shape)
+    return jnp.where(x == 0, jnp.concatenate([mine, got]), jnp.concatenate([got, mine]))
+
+
+def per_device_fast(
+    hidden_in,
+    memory,
+    src_len,
+    out_grad,
+    w_self_qkv,
+    w_self_out,
+    w_cross_q,
+    w_cross_kv,
+    w_cross_out,
+    w_ffn_in,
+    w_ffn_out,
+    biases,
+    ffn_bias,
+    norm_gain,
+    norm_shift,
+):
+    nb = lax.axis_size("batch")
+    width = hidden_in.shape[2]
+    half = width // 2
+    x, b = lax.axis_index("seq"), lax.axis_index("batch")
+    place = jnp.stack([x, b // 4, (b // 2) % 2, b % 2]).astype(jnp.int32)
+    length = lax.dynamic_slice_in_dim(src_len, x, 1)
+
+    pairs, other = split_pairs(hidden_in)
+    got = swap(other)
+    memory_pairs, memory_other = split_pairs(memory)
+    memory_got = swap(memory_other)
+    cot_pairs, cot_other = split_pairs(out_grad)
+    tokens, query_self, key_self, value_self = project(
+        place, pairs, got, w_self_qkv, biases, ((0, 0.125), (None, 1.0), (1, 1.0))
+    )
+    query_self, cot_other = tie(query_self, cot_other)
+    cot_got = swap(cot_other)
+    out_self, lp_self = attn_fwd(length, query_self, key_self, value_self, True)
+    unit_one, scale_one, low_one, query_cross = after_self(
+        out_self, tokens, w_self_out, w_cross_q, biases, norm_gain, norm_shift
+    )
+    sources, key_cross, value_cross = project(
+        place, memory_pairs, memory_got, w_cross_kv, biases, ((None, 1.0), (4, 1.0))
+    )
+    out_cross, lp_cross = attn_fwd(length, query_cross, key_cross, value_cross, False)
+    cotangent = whole_sequence(cot_pairs, cot_got)
+    layer, active, grad_pre, low_two, branch_three, grad_two, branch_two, grad_mixed, sums_ffn, bias_sums = ffn(
+        out_cross, unit_one, cotangent, w_cross_out, w_ffn_in, w_ffn_out, biases, ffn_bias[None], norm_gain, norm_shift
+    )
+    span = layer.shape[0] // 2
+
+    one = tall_grad(place, active, branch_three, nb)
+    one, low_two = tie(one, low_two)
+    one = core_stage(one, nb)
+    two = wide_grad(place, [(low_two, grad_pre, None), (out_cross, branch_two, None)], nb)
+
+    two, one, grad_mixed = tie(two, one, grad_mixed)
+    two = core_stage(two, nb)
+    one_out, one = y_prepare(one)
+    one_out, grad_mixed = tie(one_out, grad_mixed)
+    one = one + (y_move(one_out, nb),)
+    back = partial(attn_bwd, length, query_cross, key_cross, value_cross, out_cross)
+    cross_a, sums_ca = back(grad_mixed, lp_cross, False, 0, 1, 3)
+
+    cross_a, two, grad_mixed = tie(cross_a, two, grad_mixed)
+    two_out, two = y_prepare(two)
+    layer_other = lax.dynamic_slice_in_dim(layer, (1 - x) * span, span, 0)
+    two_out, layer_other, grad_mixed = tie(two_out, layer_other, grad_mixed)
+    two = two + (y_move(two_out, nb),)
+    layer_got = swap(layer_other)
+    cross_b, sums_cb = back(grad_mixed, lp_cross, False, 3, 1, 3)
+
+    cross_b, one = tie(cross_b, one)
+    one_keep, one_out = x_prepare(one)
+    one_out, cross_b = tie(one_out, cross_b)
+    one = one_keep, x_move(one_out, nb)
+    grad_one, branch_one, grad_mixed, gq_cross, sums_one = before_self(
+        grad_two, cross_a, cross_b, unit_one, scale_one, w_cross_q, w_self_out, norm_gain
+    )
+    three = wide_grad(
+        place,
+        [(out_self, branch_one, None), (low_one, gq_cross, None), (sources, cross_a, (1, 2)), (sources, cross_b, (1, 2))],
+        nb,
+    )
+
+    three, cross_a, one = tie(three, cross_a, one)
+    three = core_stage(three, nb)
+    one_keep, one_out = z_prepare(one)
+    one_out, cross_a = tie(one_out, cross_a)
+    one = one_keep, z_move(one_out, nb, 0)
+    spots = [((), ((0, 384),), ((width, 384),)), ((), ((384, 384),), ((width + 384, 384),))]
+    other = grad_rows(place, [cross_a, cross_b], spots, w_cross_kv, None, False)
+
+    other, three, two, grad_mixed = tie(other, three, two, grad_mixed)
+    three_out, three = y_prepare(three)
+    two_keep, two_out = x_prepare(two)
+    three_out, two_out, grad_mixed = tie(three_out, two_out, grad_mixed)
+    three = three + (y_move(three_out, nb),)
+    two = two_keep, x_move(two_out, nb)
+    memory_back = swap(other)
+    back = partial(attn_bwd, length, query_self, key_self, value_self, out_self)
+    self_a, sums_sa, *four = back(
+        grad_mixed, lp_self, True, 0, 3, 2, tokens, place, nb, "early", (sums_one, sums_ca, sums_cb, sums_ffn, bias_sums)
+    )
+
+    self_a, four, one, cross_a = tie(self_a, four, one, cross_a)
+    four = core_stage(four, nb)
+    one_keep, one_out = z_prepare(one)
+    one_out, cross_a = tie(one_out, cross_a)
+    one = one_keep, z_move(one_out, nb, 1)
+    memory_mine = grad_rows(place, [cross_a, cross_b], spots, w_cross_kv, None, True)
+
+    two, four, grad_mixed, memory_mine = tie(two, four, grad_mixed, memory_mine)
+    four_out, four = y_prepare(four)
+    two_keep, two_out = z_prepare(two)
+    two_out, four_out, grad_mixed = tie(two_out, four_out, grad_mixed)
+    four = four + (y_move(four_out, nb),)
+    two = two_keep, z_move(two_out, nb, 0)
+    self_b, sums_sb, *five = back(grad_mixed, lp_self, True, 1, 3, 2, tokens, place, nb)
+
+    self_b, five, three, two, grad_mixed = tie(self_b, five, three, two, grad_mixed)
+    five = core_stage(five, nb)
+    three_keep, three_out = x_prepare(three)
+    two_keep, two_out = z_prepare(two)
+    three_out, two_out, grad_mixed = tie(three_out, two_out, grad_mixed)
+    three = three_keep, x_move(three_out, nb)
+    two = two_keep, z_move(two_out, nb, 1)
+    self_c, sums_sc, *six = back(grad_mixed, lp_self, True, 2, 3, 2, tokens, place, nb, "late", (sums_sa, sums_sb))
+
+    self_c, six, five, four, three = tie(self_c, six, five, four, three)
+    six = core_stage(six, nb)
+    five_out, five = y_prepare(five)
+    four_keep, four_out = x_prepare(four)
+    three_keep, three_out = z_prepare(three)
+    five_out, four_out, three_out, self_c = tie(five_out, four_out, three_out, self_c)
+    five = five + (y_move(five_out, nb),)
+    four = four_keep, x_move(four_out, nb)
+    three = three_keep, z_move(three_out, nb, 0)
+    spots = [tuple(tuple((m * width + (i + s) * 128, 128) for s in (0, 3)) for m in range(3)) for i in range(3)]
+    other = grad_rows(place, [self_a, self_b, self_c], spots, w_self_qkv, grad_one, False)
+
+    other, six, grad_one = tie(other, six, grad_one)
+    six_out, six = y_prepare(six)
+    six_out, other, grad_one = tie(six_out, other, grad_one)
+    six = six + (y_move(six_out, nb),)
+    in_back = swap(other)
+    mine = grad_rows(place, [self_a, self_b, self_c], spots, w_self_qkv, grad_one, True)
+
+    mine, six, five, four, three, layer_got, memory_back = tie(mine, six, five, four, three, layer_got, memory_back)
+    six_out = after_y(six)
+    five_out = after_y(five)
+    both = jnp.concatenate([six_out, five_out], axis=2)
+    both = direct_z(both, nb)
+    four_keep, four_out = z_prepare(four)
+    three_keep, three_out = z_prepare(three)
+    four = four_keep, z_move(four_out, nb, 0)
+    three = three_keep, z_move(three_out, nb, 1)
+    layer_out = join_pairs(lax.dynamic_slice_in_dim(layer, x * span, span, 0), layer_got)
+    grad_memory = join_pairs(memory_mine, memory_back)
+    both = both[0] + x_move(both[1].astype(bf16), nb).astype(f32)
+    four_keep, four_out = z_prepare(four)
+    four = last_stage((four_keep, z_move(four_out, nb, 1)))
+    grad_in = join_pairs(mine, in_back)
+    group = last_stage(three)
+    grad_ffn_out = last_stage(one)
+    grad_ffn_in = last_stage(two)
+    unit = width // nb
+    ends = unit, both.shape[0] - unit
+    thirds = [s.reshape(unit, 3, 128) for s in (four[:unit], both[ends[1] :], both[: ends[0]])]
+    grad_self_qkv = jnp.stack(thirds, axis=2).reshape(unit, 9 * 128)
+    late = both[ends[0] : ends[0] + 6, :256].reshape(3, 2, 2, 128)
+    late = at(late, x, 2).swapaxes(0, 1).reshape(2, half)
+    early = lax.dynamic_slice_in_dim(four[unit:], x * 16, 16, 0)
+    vectors = jnp.concatenate([late, early[:11]])
+    bias_total = early[11 : 11 + bias_sums.shape[1] // width].reshape(-1)
+    return (
+        layer_out,
+        grad_in,
+        grad_memory,
+        grad_self_qkv,
+        group[:, :half],
+        group[:, half : 2 * half],
+        group[:, 2 * half :],
+        grad_ffn_in[:, -half:],
+        grad_ffn_in[:, :-half],
+        grad_ffn_out,
+        vectors[0:7],
+        bias_total,
+        vectors[7:10],
+        vectors[10:13],
+    )
+
+
 def solution(mesh):
+    devices = dict(mesh.shape)
+
     in_specs = (
         P("seq", "batch", None),
         P("seq", "batch", None),
@@ -495,6 +1453,12 @@
         P(None, "seq"),
         P(None, "seq"),
     )
+    nb, ns = devices["batch"], devices["seq"]
+
+    def per_device(hidden_in, *rest):
+        whole = ns == 2 and hidden_in.shape[1] == 2 and nb % 4 == 0 and nb & (nb - 1) == 0
+        return (per_device_fast if whole else per_device_general)(hidden_in, *rest)
+
     return jax.shard_map(
         per_device, mesh=mesh, in_specs=in_specs, out_specs=out_specs, check_vma=False
     )

time: 1910 us -> 429 us (0.22)
  waiting for transfers between devices: 729 us -> 68.5 us
  matrix products: 523 us -> 0 us
  local copies, waits for them, and re-layouts: 422 us -> 39.5 us
  Pallas kernels: 0 us -> 244 us
  other arithmetic: 135 us -> 31 us
  blocking collectives: 53.4 us -> 0 us
    dot_general x49 -> x0, matrix products: 523 us -> none  [the longest x4 73.3 us: block_backward(): jnp.einsum('qshd,kshd->shqk', grad_heads, value_heads, preferred_element_...]
    reduce_scatter x8 -> x0, waiting for transfers between devices: 269 us -> none  [the longest x1 64 us: per_device(): lax.psum_scatter(grad_ffn_out.astype(jnp.bfloat16), 'batch', scatter_dime...]
    pallas_call x0 -> x19, Pallas kernels: none -> 244 us  [the longest x5 80.9 us: attn_bwd(): pl.pallas_call(functools.partial(bwd_kernel, causal=causal, qb=qb, first_...]
    ppermute x12 -> x34, waiting for transfers between devices: 266 us -> 68.5 us  [the longest x28 57 us: send(): return lax.ppermute(value, ('batch', 'seq'), route(nb, move))]
    unnamed x28 -> x0, waiting for transfers between devices: 193 us -> none
    reduce_sum x17 -> x0, other arithmetic: 81.2 us -> none  [the longest x4 43 us: block(): total = total * rescale + jnp.sum(weights, axis=-1)]
    another operation x26 -> x4, local copies, waits for them, and re-layouts: 84.3 us -> 3.13 us  [per_device_fast(): grad_self_qkv = jnp.stack(thirds, axis=2).reshape(unit, 9 * 128)]
    convert_element_type x15 -> x5, local copies, waits for them, and re-layouts: 73.6 us -> 2.16 us  [the longest x4 1.51 us: x_prepare(): return (total[0].astype(bf16), total[1].astype(bf16))]
  transfers between devices with their start and end apart: 32 -> 34, of which waited for: 15 -> 6; matrix products, arithmetic and copies ran while one was open for 34% -> 11% of each run, Pallas kernels for 0% -> 46%
where the time goes in v1:
time: 429 us; the launch traced here: 421 us
  Pallas kernels  244 us (57%)
  waiting for transfers between devices  68.5 us (16%)
  local copies, waits for them, and re-layouts  39.5 us (9%)
  starting transfers between devices  35.7 us (8%)
  other arithmetic  31 us (7%)
    pallas_call x5, Pallas kernels, attn_bwd(): pl.pallas_call(functools.partial(bwd_kernel, causal=causal, qb=qb, first_...  80.9 us
    ppermute x28, waiting for transfers between devices, send(): return lax.ppermute(value, ('batch', 'seq'), route(nb, move))  57 us
    pallas_call x1, Pallas kernels, ffn(): pl.pallas_call(functools.partial(ffn_kernel, chunk=chunk), grid=(n // row...  42 us
    pallas_call x2, Pallas kernels, attn_fwd(): pl.pallas_call(functools.partial(fwd_kernel, causal=causal, heads=d // HD...  36.4 us
    ppermute x28, starting transfers between devices, send(): return lax.ppermute(value, ('batch', 'seq'), route(nb, move))  27.9 us
    pallas_call x2, Pallas kernels, wide_grad(): pl.pallas_call(functools.partial(wide_kernel, steps=steps, unit=unit), gr...  25.7 us
    pallas_call x4, Pallas kernels, grad_rows(): pl.pallas_call(functools.partial(grad_rows_kernel, columns=columns, based...  19.6 us
    pallas_call x2, Pallas kernels, project(): pl.pallas_call(functools.partial(project_kernel, step=step, plan=plan), g...  13.6 us
  transfers between devices with their start and end apart: 34, of which 6 were waited for; matrix products, arithmetic and copies ran while one was open for 11% of the time, Pallas kernels for 46%

profile of v1, /device:TPU:8, one launch (start us, length us, event | category | flops | bytes accessed | tf_op | source)
XLA Modules:
  0.0 420.9 jit_solution(7446635552187043068)
XLA Ops:
  0.7 1.7 copy.42
  3.3 1.5 collective-permute-start
  5.1 1.1 constant_dynamic-slice_fusion.4
  6.2 1.3 collective-permute-start.1
  7.4 3.0 copy.43
  11.1 1.5 constant_dynamic-slice_fusion.3
  12.6 11.5 %collective-permute-done.got = bf16[512,768]{1,0:T(8,128)(2,1)} collective-permute-done((bf16[512,768]{1,0:T(8,128)(2,1)}, bf16[512,768]{1,0:T(8,128)(2,1)}, u32[]{:S(2)}, u32[]{:S(2)}) %collective-permute-start) | collective-permute-done | bytes 786464 | tf_op jit(solution)/shard_map/ppermute | solution.py:1206
  24.1 7.1 %project.2 = (bf16[1024,768]{1,0:T(8,128)(2,1)}, bf16[1024,768]{1,0:T(8,128)(2,1)}, bf16[1024,768]{1,0:T(8,128)(2,1)}, bf16[1024,768]{1,0:T(8,128)(2,1)}) custom-call(s32[4]{0:T(128)S(1)} %pad_add_fusion.place.rest_0_, bf16[512,1536]{1,0:T(8,128)(2,1)} %bitcast.112, bf16[512,768]{1,0:T(8,128)(2,1)} %collective-permute-done.got, ...), custom_call_target="tpu_custom_call" | custom-call | flops 3623878656 | bytes 8257536 | tf_op jit(solution)/shard_map/project/pallas_call | solution.py:768
  31.1 1.5 collective-permute-start.2
  32.6 14.8 %attn_fwd.2 = (bf16[1024,768]{1,0:T(8,128)(2,1)}, bf16[1024,128]{1,0:T(8,128)(2,1)}) custom-call(s32[1]{0:T(128)} %dynamic_slice.28.len_ref, bf16[1024,768]{1,0:T(8,128)(2,1)} %get-tuple-element.171.q_ref, bf16[1024,768]{1,0:T(8,128)(2,1)} %get-tuple-element.172.k_ref, bf16[1024,768]{1,0:T(8,128)(2,1)} %get-tuple-element.173.v_ref), custom_call_target="tpu_custom_call" | custom-call | flops 8053063680 | bytes 6291456 | tf_op jit(solution)/shard_map/attn_fwd/pallas_call | solution.py:550
  47.4 7.4 %after_self.1 = (f32[1024,768]{1,0:T(8,128)}, f32[1024,128]{1,0:T(8,128)}, bf16[1024,768]{1,0:T(8,128)(2,1)}, bf16[1024,768]{1,0:T(8,128)(2,1)}) custom-call(bf16[1024,768]{1,0:T(8,128)(2,1)} %get-tuple-element.174.o.refs_0_.o_ref, bf16[1024,768]{1,0:T(8,128)(2,1)} %get-tuple-element.175.tok.rest_1_, bf16[768,768]{1,0:T(8,128)(2,1)S(1)} %copy-done.4, ...), custom_call_target="tpu_custom_call" | custom-call | flops 2415919104 | bytes 11796480 | tf_op jit(solution)/shard_map/after_self/pallas_call | solution.py:821
  54.9 6.5 %project.3 = (bf16[1024,768]{1,0:T(8,128)(2,1)}, bf16[1024,768]{1,0:T(8,128)(2,1)}, bf16[1024,768]{1,0:T(8,128)(2,1)}) custom-call(s32[4]{0:T(128)S(1)} %pad_add_fusion.place.rest_0_, bf16[512,1536]{1,0:T(8,128)(2,1)} %bitcast.110, bf16[512,768]{1,0:T(8,128)(2,1)} %collective-permute-done.1.got, bf16[768,1536]{1,0:T(8,128)(2,1)S(1)} %copy-done.1, ...), custom_call_target="tpu_custom_call" | custom-call | flops 2415919104 | bytes 7077888 | tf_op jit(solution)/shard_map/project/pallas_call | solution.py:768
  61.4 21.6 %attn_fwd.3 = (bf16[1024,768]{1,0:T(8,128)(2,1)}, bf16[1024,128]{1,0:T(8,128)(2,1)}) custom-call(s32[1]{0:T(128)} %dynamic_slice.28.len_ref, bf16[1024,768]{1,0:T(8,128)(2,1)} %get-tuple-element.176.q_ref, bf16[1024,768]{1,0:T(8,128)(2,1)} %get-tuple-element.177.k_ref, bf16[1024,768]{1,0:T(8,128)(2,1)} %get-tuple-element.178.v_ref), custom_call_target="tpu_custom_call" | custom-call | flops 16106127360 | bytes 6291456 | tf_op jit(solution)/shard_map/attn_fwd/pallas_call | solution.py:550
  83.1 1.8 maximum_select_fusion.cot
  84.9 42.0 %ffn.1 = (bf16[1024,768]{1,0:T(8,128)(2,1)}, bf16[1024,3072]{1,0:T(8,128)(2,1)}, bf16[1024,3072]{1,0:T(8,128)(2,1)}, bf16[1024,768]{1,0:T(8,128)(2,1)}, bf16[102...) custom-call(bf16[1024,768]{1,0:T(8,128)(2,1)} %get-tuple-element.179, ...), custom_call_target="tpu_custom_call" | custom-call | flops 21743271936 | bytes 37748736 | tf_op jit(solution)/shard_map/ffn/pallas_call | solution.py:934
  126.9 10.2 %tall_grad.1 = (bf16[2,2,4,192,384]{4,3,2,1,0:T(8,128)(2,1)}, bf16[2,2,4,192,384]{4,3,2,1,0:T(8,128)(2,1)}) custom-call(s32[4]{0:T(128)S(1)} %pad_add_fusion.place.rest_0_, bf16[1024,3072]{1,0:T(8,128)(2,1)} %get-tuple-element.184.a, bf16[1024,768]{1,0:T(8,128)(2,1)} %get-tuple-element.185.b), custom_call_target="tpu_custom_call" | custom-call | flops 4831838208 | bytes 12582912 | tf_op jit(solution)/shard_map/tall_grad/pallas_call | solution.py:1028
  137.1 13.3 %wide_grad.2 = (bf16[2,2,4,48,1920]{4,3,2,1,0:T(8,128)(2,1)}, bf16[2,2,4,48,1920]{4,3,2,1,0:T(8,128)(2,1)}) custom-call(s32[4]{0:T(128)S(1)} %pad_add_fusion.place.rest_0_, bf16[1024,768]{1,0:T(8,128)(2,1)} %get-tuple-element.189.refs_0_, bf16[1024,3072]{1,0:T(8,128)(2,1)} %get-tuple-element.190.refs_1_.refs_2_, ...), custom_call_target="tpu_custom_call" | custom-call | flops 6039797760 | bytes 13762560 | tf_op jit(solution)/shard_map/wide_grad/pallas_call | solution.py:1076
  151.0 2.1 constant_dynamic-slice_fusion.2
  153.0 1.9 fusion.4
  154.9 1.6 collective-permute-start.5
  156.5 18.8 %attn_bwd.5 = (bf16[3,1024,384]{2,1,0:T(8,128)(2,1)}, f32[8,384]{1,0:T(8,128)}) custom-call(s32[1]{0:T(128)} %dynamic_slice.28.len_ref, bf16[1024,768]{1,0:T(8,128)(2,1)} %get-tuple-element.176.q_ref, bf16[1024,768]{1,0:T(8,128)(2,1)} %get-tuple-element.177.k_ref, bf16[1024,768]{1,0:T(8,128)(2,1)} %get-tuple-element.178.v_ref, ...), custom_call_target="tpu_custom_call" | custom-call | flops 20132659200 | bytes 6291456 | tf_op jit(solution)/shard_map/attn_bwd/pallas_call | solution.py:713
  175.4 1.7 fusion.3
  177.1 19.2 %attn_bwd.6 = (bf16[3,1024,384]{2,1,0:T(8,128)(2,1)}, f32[8,384]{1,0:T(8,128)}) custom-call(s32[1]{0:T(128)} %dynamic_slice.28.len_ref, bf16[1024,768]{1,0:T(8,128)(2,1)} %get-tuple-element.176.q_ref, bf16[1024,768]{1,0:T(8,128)(2,1)} %get-tuple-element.177.k_ref, bf16[1024,768]{1,0:T(8,128)(2,1)} %get-tuple-element.178.v_ref, ...), custom_call_target="tpu_custom_call" | custom-call | flops 20132659200 | bytes 6291456 | tf_op jit(solution)/shard_map/attn_bwd/pallas_call | solution.py:713
  196.3 1.8 fusion.2
  199.7 8.3 %before_self.1 = (f32[1024,768]{1,0:T(8,128)}, bf16[1024,768]{1,0:T(8,128)(2,1)}, bf16[1024,768]{1,0:T(8,128)(2,1)}, bf16[1024,768]{1,0:T(8,128)(2,1)}, f32[8,768]{1,0:T(8,128)}) custom-call(f32[1024,768]{1,0:T(8,128)} %get-tuple-element.183.g2, bf16[3,1024,384]{2,1,0:T(8,128)(2,1)} %get-tuple-element.257.gqa.refs_7_.refs_8_.refs_0_, ...), custom_call_target="tpu_custom_call" | custom-call | flops 2415919104 | bytes 16515072 | tf_op jit(solution)/shard_map/before_self/pallas_call | solution.py:981
  208.0 12.5 %wide_grad.3 = (bf16[2,2,4,48,1536]{4,3,2,1,0:T(8,128)(2,1)}, bf16[2,2,4,48,1536]{4,3,2,1,0:T(8,128)(2,1)}) custom-call(s32[4]{0:T(128)S(1)} %pad_add_fusion.place.rest_0_, bf16[1024,768]{1,0:T(8,128)(2,1)} %get-tuple-element.174.o.refs_0_.o_ref, bf16[1024,768]{1,0:T(8,128)(2,1)} %get-tuple-element.218.refs_1_.refs_2_, ...), custom_call_target="tpu_custom_call" | custom-call | flops 4831838208 | bytes 11010048 | tf_op jit(solution)/shard_map/wide_grad/pallas_call | solution.py:1076
  222.1 4.6 %grad_rows.4 = bf16[512,768]{1,0:T(8,128)(2,1)} custom-call(s32[4]{0:T(128)S(1)} %pad_add_fusion.place.rest_0_, bf16[3,1024,384]{2,1,0:T(8,128)(2,1)} %get-tuple-element.257.gqa.refs_7_.refs_8_.refs_0_, bf16[3,1024,384]{2,1,0:T(8,128)(2,1)} %get-tuple-element.216.gqb.refs_9_.refs_10_.refs_1_, bf16[768,1536]{1,0:T(8,128)(2,1)S(1)} %copy-done.2), custom_call_target="tpu_custom_call" | custom-call | flops 1207959552 | bytes 7077888 | tf_op jit(solution)/shard_map/grad_rows/pallas_call | solution.py:1116
  226.7 28.6 %collective-permute-done.8 = bf16[2,4,48,1920]{3,2,1,0:T(8,128)(2,1)S(1)} collective-permute-done((bf16[2,4,48,1920]{3,2,1,0:T(8,128)(2,1)S(1)}, bf16[2,4,48,1920]{3,2,1,0:T(8,128)(2,1)S(1)}, u32[]{:S(2)}, u32[]{:S(2)}) %collective-permute-start.8) | collective-permute-done | bytes 1474592 | tf_op jit(solution)/shard_map/ppermute | solution.py:1143
  255.3 2.8 fusion
  258.1 1.3 slice_bitcast_fusion
  260.2 1.3 fusion.5
  261.6 14.3 %attn_bwd.7 = (bf16[3,1024,256]{2,1,0:T(8,128)(2,1)}, f32[8,256]{1,0:T(8,128)}, bf16[2,2,4,80,384]{4,3,2,1,0:T(8,128)(2,1)}, bf16[2,2,4,80,384]{4,3,2,1,0:T(8,128)(2,1)}) custom-call(s32[1]{0:T(128)} %dynamic_slice.28.len_ref, bf16[1024,768]{1,0:T(8,128)(2,1)} %get-tuple-element.171.q_ref, bf16[1024,768]{1,0:T(8,128)(2,1)} %get-tuple-element.172.k_ref, ...), custom_call_target="tpu_custom_call" | custom-call | flops 6710886400 | bytes 4194304 | tf_op jit(solution)/shard_map/attn_bwd/pallas_call | solution.py:713
  278.1 2.6 collective-permute-start.33
  280.7 1.4 collective-permute-start.22
  282.6 1.7 copy-done.3
  284.3 4.7 %grad_rows.5 = f32[512,768]{1,0:T(8,128)} custom-call(s32[4]{0:T(128)S(1)} %pad_add_fusion.place.rest_0_, bf16[3,1024,384]{2,1,0:T(8,128)(2,1)} %get-tuple-element.257.gqa.refs_7_.refs_8_.refs_0_, bf16[3,1024,384]{2,1,0:T(8,128)(2,1)} %get-tuple-element.216.gqb.refs_9_.refs_10_.refs_1_, bf16[768,1536]{1,0:T(8,128)(2,1)S(1)} %copy-done.3), custom_call_target="tpu_custom_call" | custom-call | flops 1207959552 | bytes 7077888 | tf_op jit(solution)/shard_map/grad_rows/pallas_call | solution.py:1116
  289.7 1.7 add_bitcast_fusion.1
  291.4 4.3 %collective-permute-done.10 = bf16[4,48,1920]{2,1,0:T(8,128)(2,1)} collective-permute-done((bf16[4,48,1920]{2,1,0:T(8,128)(2,1)}, bf16[4,48,1920]{2,1,0:T(8,128)(2,1)}, u32[]{:S(2)}, u32[]{:S(2)}) %collective-permute-start.10) | collective-permute-done | bytes 737312 | tf_op jit(solution)/shard_map/ppermute | solution.py:1143
  295.6 1.3 add_convert_fusion.3
  296.9 1.2 fusion.9
  299.2 14.5 %attn_bwd.8 = (bf16[3,1024,256]{2,1,0:T(8,128)(2,1)}, f32[8,256]{1,0:T(8,128)}, bf16[2,2,4,48,384]{4,3,2,1,0:T(8,128)(2,1)}, bf16[2,2,4,48,384]{4,3,2,1,0:T(8,128)(2,1)}) custom-call(s32[1]{0:T(128)} %dynamic_slice.28.len_ref, bf16[1024,768]{1,0:T(8,128)(2,1)} %get-tuple-element.171.q_ref, bf16[1024,768]{1,0:T(8,128)(2,1)} %get-tuple-element.172.k_ref, ...), custom_call_target="tpu_custom_call" | custom-call | flops 6710886400 | bytes 4194304 | tf_op jit(solution)/shard_map/attn_bwd/pallas_call | solution.py:713
  315.3 14.1 %attn_bwd.9 = (bf16[3,1024,256]{2,1,0:T(8,128)(2,1)}, f32[8,256]{1,0:T(8,128)}, bf16[2,2,4,64,384]{4,3,2,1,0:T(8,128)(2,1)}, bf16[2,2,4,64,384]{4,3,2,1,0:T(8,128)(2,1)}) custom-call(s32[1]{0:T(128)} %dynamic_slice.28.len_ref, bf16[1024,768]{1,0:T(8,128)(2,1)} %get-tuple-element.171.q_ref, bf16[1024,768]{1,0:T(8,128)(2,1)} %get-tuple-element.172.k_ref, ...), custom_call_target="tpu_custom_call" | custom-call | flops 6710886400 | bytes 4194304 | tf_op jit(solution)/shard_map/attn_bwd/pallas_call | solution.py:713
  329.5 2.6 collective-permute-start.32
  332.1 9.3 %collective-permute-done.16 = bf16[4,48,1536]{2,1,0:T(8,128)(2,1)S(1)} collective-permute-done((bf16[4,48,1536]{2,1,0:T(8,128)(2,1)S(1)}, bf16[4,48,1536]{2,1,0:T(8,128)(2,1)S(1)}, u32[]{:S(2)}, u32[]{:S(2)}) %collective-permute-start.16) | collective-permute-done | bytes 589856 | tf_op jit(solution)/shard_map/ppermute | solution.py:1143
  341.7 1.3 fusion.6
  343.7 5.1 %grad_rows.6 = bf16[512,768]{1,0:T(8,128)(2,1)} custom-call(s32[4]{0:T(128)S(1)} %pad_add_fusion.place.rest_0_, bf16[3,1024,256]{2,1,0:T(8,128)(2,1)} %get-tuple-element.250.refs_0_, bf16[3,1024,256]{2,1,0:T(8,128)(2,1)} %get-tuple-element.269.refs_1_, bf16[3,1024,256]{2,1,0:T(8,128)(2,1)} %get-tuple-element.294.refs_2_, bf16[768,2304]{1,0:T(8,128)(2,1)S(1)} %copy-done, ...), custom_call_target="tpu_custom_call" | custom-call | flops 1811939328 | bytes 9043968 | tf_op jit(solution)/shard_map/grad_rows/pallas_call | solution.py:1116
  350.1 1.5 collective-permute-start.18
  353.1 5.2 %grad_rows.7 = f32[512,768]{1,0:T(8,128)} custom-call(s32[4]{0:T(128)S(1)} %pad_add_fusion.place.rest_0_, bf16[3,1024,256]{2,1,0:T(8,128)(2,1)} %get-tuple-element.250.refs_0_, bf16[3,1024,256]{2,1,0:T(8,128)(2,1)} %get-tuple-element.269.refs_1_, bf16[3,1024,256]{2,1,0:T(8,128)(2,1)} %get-tuple-element.294.refs_2_, bf16[768,2304]{1,0:T(8,128)(2,1)S(1)} %copy-done, ...), custom_call_target="tpu_custom_call" | custom-call | flops 1811939328 | bytes 9043968 | tf_op jit(solution)/shard_map/grad_rows/pallas_call | solution.py:1116
  358.3 1.5 collective-permute-start.24
  359.8 1.2 collective-permute-done.18
  361.9 1.4 collective-permute-start.25
  365.0 2.6 collective-permute-start.28
  368.7 1.3 reshape.123
  370.0 3.5 collective-permute-start.31
  374.5 13.6 %collective-permute-done.31 = bf16[1,48,1536]{2,1,0:T(8,128)(2,1)S(1)} collective-permute-done((bf16[1,48,1536]{2,1,0:T(8,128)(2,1)S(1)}, bf16[1,48,1536]{2,1,0:T(8,128)(2,1)S(1)}, u32[]{:S(2)}, u32[]{:S(2)}) %collective-permute-start.31) | collective-permute-done | bytes 147488 | tf_op jit(solution)/shard_map/ppermute | solution.py:1143
  388.1 3.4 collective-permute-start.26
  392.9 1.2 fusion.12
  396.8 1.6 stack_reshape.9
  404.7 1.8 reshape.126
  406.5 1.3 pad_maximum_fusion.5
  407.8 3.4 convert_select_fusion.1
  411.6 3.3 reshape.125
  414.9 2.2 pad_maximum_fusion
  417.1 3.3 reshape.124
  (193 shorter events, 32.0 us)
Async XLA Ops:
  2.3 2.5 copy-start.16
  3.3 20.7 %collective-permute-start = (bf16[512,768]{1,0:T(8,128)(2,1)}, bf16[512,768]{1,0:T(8,128)(2,1)}, u32[]{:S(2)}, u32[]{:S(2)}) collective-permute-start(bf16[512,768]{1,0:T(8,128)(2,1)} %constant_dynamic-slice_fusion.6), channel_id=1, source_target_pairs={{0,1},{1,0},{2,3},{3,2},{4,5},{5,4},{6,7},{7,6},{8,9},{9,8},{10,11... | collective-permute-start | bytes 2359304 | tf_op jit(solution)/shard_map/ppermute | solution.py:1206
  5.1 5.3 %copy-start.42 = (s32[2]{0:T(128)S(1)}, s32[2]{0:T(128)}, u32[]{:S(2)}) copy-start(s32[2]{0:T(128)} %param.17) | copy-start | bytes 28
  6.2 48.7 %collective-permute-start.1 = (bf16[512,768]{1,0:T(8,128)(2,1)}, bf16[512,768]{1,0:T(8,128)(2,1)}, u32[]{:S(2)}, u32[]{:S(2)}) collective-permute-start(bf16[512,768]{1,0:T(8,128)(2,1)} %constant_dynamic-slice_fusion.4), channel_id=1, source_target_pairs={{0,1},{1,0},{2,3},{3,2},{4,5},{5,4},{6,7},{7,6},{8,9},{9,8},{10,11... | collective-permute-start | bytes 2359304 | tf_op jit(solution)/shard_map/ppermute | solution.py:1206
  7.4 16.6 %copy-start = (bf16[768,2304]{1,0:T(8,128)(2,1)S(1)}, bf16[768,2304]{1,0:T(8,128)(2,1)}, u32[]{:S(2)}) copy-start(bf16[768,2304]{1,0:T(8,128)(2,1)} %refs_3_.3) | copy-start | bytes 10616836
  11.1 13.0 %copy-start.10 = (f32[7,768]{1,0:T(8,128)S(1)}, f32[7,768]{1,0:T(8,128)}, u32[]{:S(2)}) copy-start(f32[7,768]{1,0:T(8,128)} %biases.7) | copy-start | bytes 64516
  31.1 52.0 %collective-permute-start.2 = (bf16[512,768]{1,0:T(8,128)(2,1)S(1)}, bf16[512,768]{1,0:T(8,128)(2,1)S(1)}, u32[]{:S(2)}, u32[]{:S(2)}) collective-permute-start(bf16[512,768]{1,0:T(8,128)(2,1)S(1)} %get-tuple-element.181), channel_id=1, source_target_pairs={{0,1},{1,0},{2,3},{3,2},{4,5},{5,4},{6,7},{7,6},{8,9},{9,8},{10,11... | collective-permute-start | bytes 2359304 | tf_op jit(solution)/shard_map/ppermute | solution.py:1206
  32.6 14.8 %copy-start.4 = (bf16[768,768]{1,0:T(8,128)(2,1)S(1)}, bf16[768,768]{1,0:T(8,128)(2,1)}, u32[]{:S(2)}) copy-start(bf16[768,768]{1,0:T(8,128)(2,1)} %w_out.5) | copy-start | bytes 3538948
  32.6 14.8 %copy-start.6 = (bf16[768,768]{1,0:T(8,128)(2,1)S(1)}, bf16[768,768]{1,0:T(8,128)(2,1)}, u32[]{:S(2)}) copy-start(bf16[768,768]{1,0:T(8,128)(2,1)} %w_q.3) | copy-start | bytes 3538948
  32.6 14.8 %copy-start.8 = (f32[3,768]{1,0:T(4,128)S(1)}, f32[3,768]{1,0:T(4,128)}, u32[]{:S(2)}) copy-start(f32[3,768]{1,0:T(4,128)} %gain.5) | copy-start | bytes 27652
  32.6 14.8 %copy-start.11 = (f32[3,768]{1,0:T(4,128)S(1)}, f32[3,768]{1,0:T(4,128)}, u32[]{:S(2)}) copy-start(f32[3,768]{1,0:T(4,128)} %shift.3) | copy-start | bytes 27652
  47.4 7.4 %copy-start.1 = (bf16[768,1536]{1,0:T(8,128)(2,1)S(1)}, bf16[768,1536]{1,0:T(8,128)(2,1)}, u32[]{:S(2)}) copy-start(bf16[768,1536]{1,0:T(8,128)(2,1)} %refs_2_.3) | copy-start | bytes 7077892
  54.9 30.0 %slice-start = ((s8[4718592]{0:T(1024)(128)(4,1)}), s8[4194304]{0:T(1024)(128)(4,1)S(1)}, s32[]{:S(2)}) async-start(s8[4718592]{0:T(1024)(128)(4,1)} %bitcast.105), calls=%async_computation | async-start | bytes 8388608
  61.4 23.5 %slice-start.1 = ((s8[4718592]{0:T(1024)(128)(4,1)}), s8[524288]{0:T(1024)(128)(4,1)S(1)}, s32[]{:S(2)}) async-start(s8[4718592]{0:T(1024)(128)(4,1)} %bitcast.105), calls=%async_computation.1 | async-start | bytes 1048576
  137.1 13.3 %collective-permute-start.3 = (bf16[2,2,4,192,384]{4,3,2,1,0:T(8,128)(2,1)}, bf16[2,2,4,192,384]{4,3,2,1,0:T(8,128)(2,1)}, u32[]{:S(2)}, u32[]{:S(2)}) collective-permute-start(bf16[2,2,4,192,384]{4,3,2,1,0:T(8,128)(2,1)} %get-tuple-element.195), channel_id=1, source_target_pairs={{0,2},{1,3},{2,0},{3,1},{4,6},{5,7},{6,4},{7,5},{8,10},{9,11},{10,... | collective-permute-start | bytes 7077896 | tf_op jit(solution)/shard_map/ppermute | solution.py:1143
  150.4 25.0 %collective-permute-start.4 = (bf16[2,2,4,48,1920]{4,3,2,1,0:T(8,128)(2,1)}, bf16[2,2,4,48,1920]{4,3,2,1,0:T(8,128)(2,1)}, u32[]{:S(2)}, u32[]{:S(2)}) collective-permute-start(bf16[2,2,4,48,1920]{4,3,2,1,0:T(8,128)(2,1)} %get-tuple-element.204), channel_id=1, source_target_pairs={{0,2},{1,3},{2,0},{3,1},{4,6},{5,7},{6,4},{7,5},{8,10},{9,11},{10,... | collective-permute-start | bytes 8847368 | tf_op jit(solution)/shard_map/ppermute | solution.py:1143
  154.9 41.3 %collective-permute-start.5 = (bf16[2,4,192,384]{3,2,1,0:T(8,128)(2,1)S(1)}, bf16[2,4,192,384]{3,2,1,0:T(8,128)(2,1)S(1)}, u32[]{:S(2)}, u32[]{:S(2)}) collective-permute-start(bf16[2,4,192,384]{3,2,1,0:T(8,128)(2,1)S(1)} %fusion.4), channel_id=1, source_target_pairs={{0,4},{1,5},{2,6},{3,7},{4,0},{5,1},{6,2},{7,3},{8,12},{9,13},{10,... | collective-permute-start | bytes 3538952 | tf_op jit(solution)/shard_map/ppermute | solution.py:1143
  156.5 18.8 %copy-start.17 = (bf16[2,2,4,48,1920]{4,3,2,1,0:T(8,128)(2,1)S(1)}, bf16[2,2,4,48,1920]{4,3,2,1,0:T(8,128)(2,1)}, u32[]{:S(2)}) copy-start(bf16[2,2,4,48,1920]{4,3,2,1,0:T(8,128)(2,1)} %get-tuple-element.235) | copy-start | bytes 8847364
  177.1 19.2 %copy-start.25 = (bf16[2,2,4,192,384]{4,3,2,1,0:T(8,128)(2,1)S(1)}, bf16[2,2,4,192,384]{4,3,2,1,0:T(8,128)(2,1)}, u32[]{:S(2)}) copy-start(bf16[2,2,4,192,384]{4,3,2,1,0:T(8,128)(2,1)} %get-tuple-element.212) | copy-start | bytes 7077892
  198.2 22.3 %collective-permute-start.6 = (bf16[4,192,384]{2,1,0:T(8,128)(2,1)S(1)}, bf16[4,192,384]{2,1,0:T(8,128)(2,1)S(1)}, u32[]{:S(2)}, u32[]{:S(2)}) collective-permute-start(bf16[4,192,384]{2,1,0:T(8,128)(2,1)S(1)} %get-tuple-element.224), channel_id=1, source_target_pairs={{0,1},{1,0},{2,3},{3,2},{4,5},{5,4},{6,7},{7,6},{8,9},{9,8},{10,11... | collective-permute-start | bytes 1769480 | tf_op jit(solution)/shard_map/ppermute | solution.py:1143
  220.5 34.8 %collective-permute-start.7 = (bf16[2,2,4,48,1536]{4,3,2,1,0:T(8,128)(2,1)}, bf16[2,2,4,48,1536]{4,3,2,1,0:T(8,128)(2,1)S(1)}, u32[]{:S(2)}, u32[]{:S(2)}) collective-permute-start(bf16[2,2,4,48,1536]{4,3,2,1,0:T(8,128)(2,1)} %get-tuple-element.230), channel_id=1, source_target_pairs={{0,2},{1,3},{2,0},{3,1},{4,6},{5,7},{6,4},{7,5},{8,10},{9,11},{10,... | collective-permute-start | bytes 7077896 | tf_op jit(solution)/shard_map/ppermute | solution.py:1143
  220.6 34.7 %collective-permute-start.8 = (bf16[2,4,48,1920]{3,2,1,0:T(8,128)(2,1)S(1)}, bf16[2,4,48,1920]{3,2,1,0:T(8,128)(2,1)S(1)}, u32[]{:S(2)}, u32[]{:S(2)}) collective-permute-start(bf16[2,4,48,1920]{3,2,1,0:T(8,128)(2,1)S(1)} %fusion.3), channel_id=1, source_target_pairs={{0,4},{1,5},{2,6},{3,7},{4,0},{5,1},{6,2},{7,3},{8,12},{9,13},{10,... | collective-permute-start | bytes 4423688 | tf_op jit(solution)/shard_map/ppermute | solution.py:1143
  221.4 54.5 %collective-permute-start.9 = (bf16[2,192,384]{2,1,0:T(8,128)(2,1)S(1)}, bf16[2,192,384]{2,1,0:T(8,128)(2,1)S(1)}, u32[]{:S(2)}, u32[]{:S(2)}) collective-permute-start(bf16[2,192,384]{2,1,0:T(8,128)(2,1)S(1)} %get-tuple-element.249), channel_id=1, source_target_pairs={{0,8},{1,9},{2,10},{3,11},{4,12},{5,13},{6,14},{7,15},{8,0},{9,1},... | collective-permute-start | bytes 884744 | tf_op jit(solution)/shard_map/ppermute | solution.py:1143
  255.3 4.0 copy-start.23
  275.9 19.8 %collective-permute-start.11 = (bf16[2,2,4,80,384]{4,3,2,1,0:T(8,128)(2,1)}, bf16[2,2,4,80,384]{4,3,2,1,0:T(8,128)(2,1)}, u32[]{:S(2)}, u32[]{:S(2)}) collective-permute-start(bf16[2,2,4,80,384]{4,3,2,1,0:T(8,128)(2,1)} %get-tuple-element.253), channel_id=1, source_target_pairs={{0,2},{1,3},{2,0},{3,1},{4,6},{5,7},{6,4},{7,5},{8,10},{9,11},{10,... | collective-permute-start | bytes 2949128 | tf_op jit(solution)/shard_map/ppermute | solution.py:1143
  275.9 19.7 %collective-permute-start.10 = (bf16[4,48,1920]{2,1,0:T(8,128)(2,1)}, bf16[4,48,1920]{2,1,0:T(8,128)(2,1)}, u32[]{:S(2)}, u32[]{:S(2)}) collective-permute-start(bf16[4,48,1920]{2,1,0:T(8,128)(2,1)} %get-tuple-element.251), channel_id=1, source_target_pairs={{0,1},{1,0},{2,3},{3,2},{4,5},{5,4},{6,7},{7,6},{8,9},{9,8},{10,11... | collective-permute-start | bytes 2211848 | tf_op jit(solution)/shard_map/ppermute | solution.py:1143
  278.1 10.9 %collective-permute-start.33 = (bf16[1,192,384]{2,1,0:T(8,128)(2,1)}, bf16[1,192,384]{2,1,0:T(8,128)(2,1)}, u32[]{:S(2)}, u32[]{:S(2)}) collective-permute-start(bf16[1,192,384]{2,1,0:T(8,128)(2,1)} %slice.330), channel_id=1, source_target_pairs={{0,16},{1,17},{2,18},{3,19},{4,20},{5,21},{6,22},{7,23},{8,24},{9,... | collective-permute-start | bytes 442376 | tf_op jit(solution)/shard_map/ppermute | solution.py:1143
  280.7 68.7 %collective-permute-start.22 = (bf16[512,768]{1,0:T(8,128)(2,1)}, bf16[512,768]{1,0:T(8,128)(2,1)S(1)}, u32[]{:S(2)}, u32[]{:S(2)}) collective-permute-start(bf16[512,768]{1,0:T(8,128)(2,1)} %constant_dynamic-slice_fusion.2), channel_id=1, source_target_pairs={{0,1},{1,0},{2,3},{3,2},{4,5},{5,4},{6,7},{7,6},{8,9},{9,8},{10,11... | collective-permute-start | bytes 2359304 | tf_op jit(solution)/shard_map/ppermute | solution.py:1206
  282.1 31.5 %collective-permute-start.12 = (bf16[2,4,48,1536]{3,2,1,0:T(8,128)(2,1)}, bf16[2,4,48,1536]{3,2,1,0:T(8,128)(2,1)S(1)}, u32[]{:S(2)}, u32[]{:S(2)}) collective-permute-start(bf16[2,4,48,1536]{3,2,1,0:T(8,128)(2,1)} %fusion.5), channel_id=1, source_target_pairs={{0,4},{1,5},{2,6},{3,7},{4,0},{5,1},{6,2},{7,3},{8,12},{9,13},{10,... | collective-permute-start | bytes 3538952 | tf_op jit(solution)/shard_map/ppermute | solution.py:1143
  284.3 4.7 %copy-start.37 = (bf16[512,768]{1,0:T(8,128)(2,1)S(1)}, bf16[512,768]{1,0:T(8,128)(2,1)}, u32[]{:S(2)}) copy-start(bf16[512,768]{1,0:T(8,128)(2,1)} %grad_rows.4) | copy-start | bytes 2359300
  284.3 5.4 %copy-start.29 = (bf16[2,192,384]{2,1,0:T(8,128)(2,1)S(1)}, bf16[2,192,384]{2,1,0:T(8,128)(2,1)}, u32[]{:S(2)}) copy-start(bf16[2,192,384]{2,1,0:T(8,128)(2,1)} %copy-done.28) | copy-start | bytes 884740
  284.3 11.3 %copy-start.18 = (bf16[4,48,1920]{2,1,0:T(8,128)(2,1)S(1)}, bf16[4,48,1920]{2,1,0:T(8,128)(2,1)}, u32[]{:S(2)}) copy-start(bf16[4,48,1920]{2,1,0:T(8,128)(2,1)} %get-tuple-element.258) | copy-start | bytes 2211844
  289.0 7.9 %copy-start.34 = (bf16[2,2,4,80,384]{4,3,2,1,0:T(8,128)(2,1)S(1)}, bf16[2,2,4,80,384]{4,3,2,1,0:T(8,128)(2,1)}, u32[]{:S(2)}) copy-start(bf16[2,2,4,80,384]{4,3,2,1,0:T(8,128)(2,1)} %get-tuple-element.288) | copy-start | bytes 2949124
  289.0 69.3 %collective-permute-start.23 = (bf16[512,768]{1,0:T(8,128)(2,1)S(1)}, bf16[512,768]{1,0:T(8,128)(2,1)S(1)}, u32[]{:S(2)}, u32[]{:S(2)}) collective-permute-start(bf16[512,768]{1,0:T(8,128)(2,1)S(1)} %copy-done.37), channel_id=1, source_target_pairs={{0,1},{1,0},{2,3},{3,2},{4,5},{5,4},{6,7},{7,6},{8,9},{9,8},{10,11... | collective-permute-start | bytes 2359304 | tf_op jit(solution)/shard_map/ppermute | solution.py:1206
  298.2 15.5 %collective-permute-start.13 = (bf16[2,48,1920]{2,1,0:T(8,128)(2,1)S(1)}, bf16[2,48,1920]{2,1,0:T(8,128)(2,1)S(1)}, u32[]{:S(2)}, u32[]{:S(2)}) collective-permute-start(bf16[2,48,1920]{2,1,0:T(8,128)(2,1)S(1)} %get-tuple-element.268), channel_id=1, source_target_pairs={{0,8},{1,9},{2,10},{3,11},{4,12},{5,13},{6,14},{7,15},{8,0},{9,1},... | collective-permute-start | bytes 1105928 | tf_op jit(solution)/shard_map/ppermute | solution.py:1143
  298.6 30.8 %collective-permute-start.15 = (bf16[2,4,80,384]{3,2,1,0:T(8,128)(2,1)S(1)}, bf16[2,4,80,384]{3,2,1,0:T(8,128)(2,1)S(1)}, u32[]{:S(2)}, u32[]{:S(2)}) collective-permute-start(bf16[2,4,80,384]{3,2,1,0:T(8,128)(2,1)S(1)} %fusion.9), channel_id=1, source_target_pairs={{0,4},{1,5},{2,6},{3,7},{4,0},{5,1},{6,2},{7,3},{8,12},{9,13},{10,... | collective-permute-start | bytes 1474568 | tf_op jit(solution)/shard_map/ppermute | solution.py:1143
  299.1 14.6 %copy-start.22 = (bf16[2,2,4,48,1536]{4,3,2,1,0:T(8,128)(2,1)S(1)}, bf16[2,2,4,48,1536]{4,3,2,1,0:T(8,128)(2,1)}, u32[]{:S(2)}) copy-start(bf16[2,2,4,48,1536]{4,3,2,1,0:T(8,128)(2,1)} %get-tuple-element.270) | copy-start | bytes 7077892
  299.2 14.6 %copy-start.24 = (bf16[2,2,4,48,1536]{4,3,2,1,0:T(8,128)(2,1)S(1)}, bf16[2,2,4,48,1536]{4,3,2,1,0:T(8,128)(2,1)}, u32[]{:S(2)}) copy-start(bf16[2,2,4,48,1536]{4,3,2,1,0:T(8,128)(2,1)} %copy-done.23) | copy-start | bytes 7077892
  314.4 27.0 %collective-permute-start.16 = (bf16[4,48,1536]{2,1,0:T(8,128)(2,1)S(1)}, bf16[4,48,1536]{2,1,0:T(8,128)(2,1)S(1)}, u32[]{:S(2)}, u32[]{:S(2)}) collective-permute-start(bf16[4,48,1536]{2,1,0:T(8,128)(2,1)S(1)} %get-tuple-element.285), channel_id=1, source_target_pairs={{0,1},{1,0},{2,3},{3,2},{4,5},{5,4},{6,7},{7,6},{8,9},{9,8},{10,11... | collective-permute-start | bytes 1769480 | tf_op jit(solution)/shard_map/ppermute | solution.py:1143
  315.3 26.1 %collective-permute-start.14 = (bf16[2,2,4,48,384]{4,3,2,1,0:T(8,128)(2,1)S(1)}, bf16[2,2,4,48,384]{4,3,2,1,0:T(8,128)(2,1)S(1)}, u32[]{:S(2)}, u32[]{:S(2)}) collective-permute-start(bf16[2,2,4,48,384]{4,3,2,1,0:T(8,128)(2,1)S(1)} %copy-done.41), channel_id=1, source_target_pairs={{0,2},{1,3},{2,0},{3,1},{4,6},{5,7},{6,4},{7,5},{8,10},{9,11},{10,... | collective-permute-start | bytes 1769480 | tf_op jit(solution)/shard_map/ppermute | solution.py:1143
  329.5 12.2 %copy-start.40 = (bf16[2,2,4,64,384]{4,3,2,1,0:T(8,128)(2,1)S(1)}, bf16[2,2,4,64,384]{4,3,2,1,0:T(8,128)(2,1)}, u32[]{:S(2)}) copy-start(bf16[2,2,4,64,384]{4,3,2,1,0:T(8,128)(2,1)} %get-tuple-element.297) | copy-start | bytes 2359300
  329.5 20.6 %collective-permute-start.32 = (bf16[1,48,1920]{2,1,0:T(8,128)(2,1)S(1)}, bf16[1,48,1920]{2,1,0:T(8,128)(2,1)S(1)}, u32[]{:S(2)}, u32[]{:S(2)}) collective-permute-start(bf16[1,48,1920]{2,1,0:T(8,128)(2,1)S(1)} %slice.332), channel_id=1, source_target_pairs={{0,16},{1,17},{2,18},{3,19},{4,20},{5,21},{6,22},{7,23},{8,24},{9,... | collective-permute-start | bytes 552968 | tf_op jit(solution)/shard_map/ppermute | solution.py:1143
  341.6 7.2 %collective-permute-start.17 = (bf16[2,2,4,64,384]{4,3,2,1,0:T(8,128)(2,1)S(1)}, bf16[2,2,4,64,384]{4,3,2,1,0:T(8,128)(2,1)S(1)}, u32[]{:S(2)}, u32[]{:S(2)}) collective-permute-start(bf16[2,2,4,64,384]{4,3,2,1,0:T(8,128)(2,1)S(1)} %copy-done.40), channel_id=1, source_target_pairs={{0,2},{1,3},{2,0},{3,1},{4,6},{5,7},{6,4},{7,5},{8,10},{9,11},{10,... | collective-permute-start | bytes 2359304 | tf_op jit(solution)/shard_map/ppermute | solution.py:1143
  343.1 16.6 %collective-permute-start.19 = (bf16[2,4,48,384]{3,2,1,0:T(8,128)(2,1)S(1)}, bf16[2,4,48,384]{3,2,1,0:T(8,128)(2,1)S(1)}, u32[]{:S(2)}, u32[]{:S(2)}) collective-permute-start(bf16[2,4,48,384]{3,2,1,0:T(8,128)(2,1)S(1)} %fusion.13), channel_id=1, source_target_pairs={{0,4},{1,5},{2,6},{3,7},{4,0},{5,1},{6,2},{7,3},{8,12},{9,13},{10,... | collective-permute-start | bytes 884744 | tf_op jit(solution)/shard_map/ppermute | solution.py:1143
  343.7 5.6 %copy-start.35 = (bf16[2,2,4,64,384]{4,3,2,1,0:T(8,128)(2,1)S(1)}, bf16[2,2,4,64,384]{4,3,2,1,0:T(8,128)(2,1)}, u32[]{:S(2)}) copy-start(bf16[2,2,4,64,384]{4,3,2,1,0:T(8,128)(2,1)} %get-tuple-element.316) | copy-start | bytes 2359300
  348.9 10.9 %collective-permute-start.21 = (bf16[2,48,1536]{2,1,0:T(8,128)(2,1)S(1)}, bf16[2,48,1536]{2,1,0:T(8,128)(2,1)S(1)}, u32[]{:S(2)}, u32[]{:S(2)}) collective-permute-start(bf16[2,48,1536]{2,1,0:T(8,128)(2,1)S(1)} %get-tuple-element.306), channel_id=1, source_target_pairs={{0,8},{1,9},{2,10},{3,11},{4,12},{5,13},{6,14},{7,15},{8,0},{9,1},... | collective-permute-start | bytes 884744 | tf_op jit(solution)/shard_map/ppermute | solution.py:1143
  349.4 10.4 %collective-permute-start.20 = (bf16[4,80,384]{2,1,0:T(8,128)(2,1)S(1)}, bf16[4,80,384]{2,1,0:T(8,128)(2,1)S(1)}, u32[]{:S(2)}, u32[]{:S(2)}) collective-permute-start(bf16[4,80,384]{2,1,0:T(8,128)(2,1)S(1)} %get-tuple-element.305), channel_id=1, source_target_pairs={{0,1},{1,0},{2,3},{3,2},{4,5},{5,4},{6,7},{7,6},{8,9},{9,8},{10,11... | collective-permute-start | bytes 737288 | tf_op jit(solution)/shard_map/ppermute | solution.py:1143
  350.1 10.9 %collective-permute-start.18 = (bf16[2,4,64,384]{3,2,1,0:T(8,128)(2,1)S(1)}, bf16[2,4,64,384]{3,2,1,0:T(8,128)(2,1)S(1)}, u32[]{:S(2)}, u32[]{:S(2)}) collective-permute-start(bf16[2,4,64,384]{3,2,1,0:T(8,128)(2,1)S(1)} %fusion.10), channel_id=1, source_target_pairs={{0,4},{1,5},{2,6},{3,7},{4,0},{5,1},{6,2},{7,3},{8,12},{9,13},{10,... | collective-permute-start | bytes 1179656 | tf_op jit(solution)/shard_map/ppermute | solution.py:1143
  358.3 10.1 %copy-start.36 = (bf16[512,768]{1,0:T(8,128)(2,1)}, bf16[512,768]{1,0:T(8,128)(2,1)S(1)}, u32[]{:S(2)}) copy-start(bf16[512,768]{1,0:T(8,128)(2,1)S(1)} %collective-permute-done.23) | copy-start | bytes 2359300
  358.3 49.5 %collective-permute-start.24 = (bf16[512,768]{1,0:T(8,128)(2,1)}, bf16[512,768]{1,0:T(8,128)(2,1)}, u32[]{:S(2)}, u32[]{:S(2)}) collective-permute-start(bf16[512,768]{1,0:T(8,128)(2,1)} %grad_rows.6), channel_id=1, source_target_pairs={{0,1},{1,0},{2,3},{3,2},{4,5},{5,4},{6,7},{7,6},{8,9},{9,8},{10,11... | collective-permute-start | bytes 2359304 | tf_op jit(solution)/shard_map/ppermute | solution.py:1206
  361.9 8.2 %collective-permute-start.25 = (bf16[2,80,384]{2,1,0:T(8,128)(2,1)}, bf16[2,80,384]{2,1,0:T(8,128)(2,1)}, u32[]{:S(2)}, u32[]{:S(2)}) collective-permute-start(bf16[2,80,384]{2,1,0:T(8,128)(2,1)} %slice.291), channel_id=1, source_target_pairs={{0,8},{1,9},{2,10},{3,11},{4,12},{5,13},{6,14},{7,15},{8,0},{9,1},... | collective-permute-start | bytes 368648 | tf_op jit(solution)/shard_map/ppermute | solution.py:1143
  363.3 4.6 %copy-start.19 = (bf16[2,4,48,384]{3,2,1,0:T(8,128)(2,1)}, bf16[2,4,48,384]{3,2,1,0:T(8,128)(2,1)S(1)}, u32[]{:S(2)}) copy-start(bf16[2,4,48,384]{3,2,1,0:T(8,128)(2,1)S(1)} %fusion.8) | copy-start | bytes 884740
  363.3 4.6 %copy-start.27 = (bf16[1024,768]{1,0:T(8,128)(2,1)S(1)}, bf16[1024,768]{1,0:T(8,128)(2,1)}, u32[]{:S(2)}) copy-start(bf16[1024,768]{1,0:T(8,128)(2,1)} %get-tuple-element.182) | copy-start | bytes 4718596
  364.3 28.5 %collective-permute-start.27 = (bf16[2,112,384]{2,1,0:T(8,128)(2,1)}, bf16[2,112,384]{2,1,0:T(8,128)(2,1)}, u32[]{:S(2)}, u32[]{:S(2)}) collective-permute-start(bf16[2,112,384]{2,1,0:T(8,128)(2,1)} %get-tuple-element.342), channel_id=1, source_target_pairs={{0,8},{1,9},{2,10},{3,11},{4,12},{5,13},{6,14},{7,15},{8,0},{9,1},... | collective-permute-start | bytes 516104 | tf_op jit(solution)/shard_map/ppermute | solution.py:1143
  365.0 27.9 %collective-permute-start.28 = (bf16[2,112,384]{2,1,0:T(8,128)(2,1)}, bf16[2,112,384]{2,1,0:T(8,128)(2,1)}, u32[]{:S(2)}, u32[]{:S(2)}) collective-permute-start(bf16[2,112,384]{2,1,0:T(8,128)(2,1)} %get-tuple-element.344), channel_id=1, source_target_pairs={{0,16},{1,17},{2,18},{3,19},{4,20},{5,21},{6,22},{7,23},{8,24},{9,... | collective-permute-start | bytes 516104 | tf_op jit(solution)/shard_map/ppermute | solution.py:1143
  367.6 25.3 %collective-permute-start.29 = (bf16[2,112,384]{2,1,0:T(8,128)(2,1)}, bf16[2,112,384]{2,1,0:T(8,128)(2,1)}, u32[]{:S(2)}, u32[]{:S(2)}) collective-permute-start(bf16[2,112,384]{2,1,0:T(8,128)(2,1)} %get-tuple-element.343), channel_id=1, source_target_pairs={{0,24},{1,25},{2,26},{3,27},{4,28},{5,29},{6,30},{7,31},{8,16},{9,... | collective-permute-start | bytes 516104 | tf_op jit(solution)/shard_map/ppermute | solution.py:1143
  368.7 4.9 %copy-start.33 = (bf16[4,80,384]{2,1,0:T(8,128)(2,1)S(1)}, bf16[4,80,384]{2,1,0:T(8,128)(2,1)}, u32[]{:S(2)}) copy-start(bf16[4,80,384]{2,1,0:T(8,128)(2,1)} %copy-done.32) | copy-start | bytes 737284
  368.7 22.8 %copy-start.31 = (bf16[2,48,1536]{2,1,0:T(8,128)(2,1)S(1)}, bf16[2,48,1536]{2,1,0:T(8,128)(2,1)}, u32[]{:S(2)}) copy-start(bf16[2,48,1536]{2,1,0:T(8,128)(2,1)} %copy-done.30) | copy-start | bytes 884740
  370.0 22.9 %copy-start.20 = (bf16[2,4,48,384]{3,2,1,0:T(8,128)(2,1)S(1)}, bf16[2,4,48,384]{3,2,1,0:T(8,128)(2,1)}, u32[]{:S(2)}) copy-start(bf16[2,4,48,384]{3,2,1,0:T(8,128)(2,1)} %copy-done.19) | copy-start | bytes 884740
  370.0 18.1 %collective-permute-start.31 = (bf16[1,48,1536]{2,1,0:T(8,128)(2,1)S(1)}, bf16[1,48,1536]{2,1,0:T(8,128)(2,1)S(1)}, u32[]{:S(2)}, u32[]{:S(2)}) collective-permute-start(bf16[1,48,1536]{2,1,0:T(8,128)(2,1)S(1)} %slice.350), channel_id=1, source_target_pairs={{0,16},{1,17},{2,18},{3,19},{4,20},{5,21},{6,22},{7,23},{8,24},{9,... | collective-permute-start | bytes 442376 | tf_op jit(solution)/shard_map/ppermute | solution.py:1143
  388.1 7.4 %collective-permute-start.26 = (bf16[1,80,384]{2,1,0:T(8,128)(2,1)S(1)}, bf16[1,80,384]{2,1,0:T(8,128)(2,1)S(1)}, u32[]{:S(2)}, u32[]{:S(2)}) collective-permute-start(bf16[1,80,384]{2,1,0:T(8,128)(2,1)S(1)} %slice.337), channel_id=1, source_target_pairs={{0,16},{1,17},{2,18},{3,19},{4,20},{5,21},{6,22},{7,23},{8,24},{9,... | collective-permute-start | bytes 184328 | tf_op jit(solution)/shard_map/ppermute | solution.py:1143
  394.7 4.9 %collective-permute-start.30 = (bf16[112,384]{1,0:T(8,128)(2,1)}, bf16[112,384]{1,0:T(8,128)(2,1)}, u32[]{:S(2)}, u32[]{:S(2)}) collective-permute-start(bf16[112,384]{1,0:T(8,128)(2,1)} %fusion.22), channel_id=1, source_target_pairs={{0,1},{1,0},{2,3},{3,2},{4,5},{5,4},{6,7},{7,6},{8,9},{9,8},{10,11... | collective-permute-start | bytes 258056 | tf_op jit(solution)/shard_map/ppermute | solution.py:1143
  395.6 12.2 %copy-start.14 = (f32[512,768]{1,0:T(8,128)S(1)}, f32[512,768]{1,0:T(8,128)}, u32[]{:S(2)}) copy-start(f32[512,768]{1,0:T(8,128)} %grad_rows.5) | copy-start | bytes 4718596
  396.2 11.6 %copy-start.13 = (f32[512,768]{1,0:T(8,128)S(1)}, f32[512,768]{1,0:T(8,128)}, u32[]{:S(2)}) copy-start(f32[512,768]{1,0:T(8,128)} %grad_rows.7) | copy-start | bytes 4718596
  (15 other events, 22.3 us)
